TPU v7x, 32 devices: a whole 2x2x4 slice. The times are simulated.
32 devices in a mesh: seq: 2 (over x), head: 4 (over y, core), dp: 4 (over z).
Axes of the slice: x: 2, y: 2, z: 4, core: 2. Of those that a mesh axis runs over, the one named last changes fastest.
Arguments:
- layer_input: bfloat16 [4, 256, 4096], P('dp', 'seq', 'head'), may hold values from -24 to 24
- head_input: bfloat16 [4, 256, 4096], P('dp', 'seq', 'head'), may hold values from -6 to 6
- in_matrix: bfloat16 [4, 256, 512], P('dp', 'seq', 'head'), may hold values from -6 to 6
- out_matrix: bfloat16 [4, 256, 512], P('dp', 'seq', 'head'), may hold values from -6 to 6
- grad_output: bfloat16 [4, 256, 4096], P('dp', 'seq', 'head'), may hold values from -0.59765625 to 0.59765625
- step_weight: bfloat16 [4096, 64], P(None, 'head'), may hold values from -0.09375 to 0.09375
- step_bias: float32 [64], P('head'), may hold values from -7 to -6
- decay_log: float32 [64], P('head'), may hold values from -6.22 to 2.78
Outputs:
- grad_heads: bfloat16 [4, 256, 4096], P('dp', 'seq', 'head')
- grad_in_matrix: bfloat16 [4, 256, 512], P('dp', 'seq', 'head')
- grad_out_matrix: bfloat16 [4, 256, 512], P('dp', 'seq', 'head')
- grad_layer_input: bfloat16 [4, 256, 4096], P('dp', 'seq', 'head')
- grad_step_weight: float32 [4096, 64], P(('seq', 'dp'), 'head')
All inputs are finite; a program needn't handle non-finite values.
Results may differ from a plain program's by a relative error of at most 0.02.
Values may be sent and summed in bfloat16 or wider, within the bound.
A program may use at most 64 MiB of HBM per device.

v0:
```python
import jax
import jax.numpy as jnp
from jax import lax
from jax.sharding import PartitionSpec as P

H = 64
P_SIZE = 64
NSTATE = 128
G = 4
BLOCK = 128


PRECISION_LEVEL = lax.Precision.HIGHEST


def prefix(value, axis, join, neutral, backward):
    count = lax.axis_size(axis)
    place = lax.axis_index(axis)
    ahead = count - 1 - place if backward else place
    gathered = jax.tree.map(
        lambda a, kind: lax.all_gather(a.astype(kind), axis), value, (jnp.bfloat16, jnp.bfloat16)
    )
    state = jax.tree.map(lambda a, e: jnp.zeros_like(a) + jnp.asarray(e, a.dtype), value, neutral)

    def one(step, state):
        source = count - 1 - step if backward else step
        return join(
            state,
            jax.tree.map(
                lambda a, own: lax.dynamic_index_in_dim(a, source, 0, False).astype(own.dtype),
                gathered,
                value,
            ),
        )

    return lax.fori_loop(0, ahead, one, state)


def block_step(carry_state, inputs):
    input_block, b_block, c_block, step_block, decay_block = inputs
    cumulated = jnp.cumsum(decay_block, axis=-1)
    block_len = cumulated.shape[-1]
    lower_mask = jnp.arange(block_len)[:, None] >= jnp.arange(block_len)[None, :]
    decay_span = jnp.exp(
        jnp.where(lower_mask, cumulated[..., :, None] - cumulated[..., None, :], -1e30)
    )
    kernel = jnp.einsum("tgn,sgn->gts", c_block, b_block, precision=PRECISION_LEVEL)
    weight_values = kernel[:, None] * decay_span * step_block[..., None, :]
    within_block = jnp.einsum(
        "idwz,zidx->widx", weight_values, input_block, precision=PRECISION_LEVEL
    )
    carried = jnp.einsum("tgn,grnp->tgrp", c_block, carry_state, precision=PRECISION_LEVEL)
    output = within_block + jnp.moveaxis(jnp.exp(cumulated), -1, 0)[..., None] * carried
    totals = cumulated[..., -1]
    inflow = jnp.exp(totals[..., None] - cumulated) * step_block
    fresh_term = jnp.einsum(
        "grs,sgn,sgrp->grnp", inflow, b_block, input_block, precision=PRECISION_LEVEL
    )
    return (jnp.exp(totals)[..., None, None] * carry_state + fresh_term, output)


def segment(x_rows, b_rows, readout_rows, step_sizes, decays, start_state):
    length = x_rows.shape[0]
    blocks = length // BLOCK

    def split_rows(values):
        return values.reshape((blocks, BLOCK) + values.shape[1:])

    def split_last(values):
        return jnp.moveaxis(values.reshape(values.shape[:-1] + (blocks, BLOCK)), -2, 0)

    final_state, outputs = lax.scan(
        block_step,
        start_state,
        (
            split_rows(x_rows),
            split_rows(b_rows),
            split_rows(readout_rows),
            split_last(step_sizes),
            split_last(decays),
        ),
    )
    return (outputs.reshape(x_rows.shape), final_state)


def join_pairs(earlier, later):
    return (earlier[0] + later[0], jnp.exp(later[0])[..., None, None] * earlier[1] + later[1])


def body(
    layer_input, head_input, in_matrix, out_matrix, grad_output, step_weight, step_bias, decay_log
):
    tokens = head_input.shape[1]
    group_count = in_matrix.shape[2] // NSTATE
    ratio = H // G
    heads_here = group_count * ratio
    whole_input = lax.all_gather(layer_input, "head", axis=2, tiled=True)[0]
    preact = jnp.dot(whole_input, step_weight, preferred_element_type=jnp.float32) + step_bias
    step_sizes = jnp.transpose(jax.nn.softplus(preact)).reshape(group_count, ratio, tokens)
    rates = jnp.exp(decay_log).reshape(group_count, ratio)
    decays = -rates[..., None] * step_sizes
    x_rows = head_input[0].astype(jnp.float32).reshape(tokens, group_count, ratio, P_SIZE)
    b_rows = in_matrix[0].astype(jnp.float32).reshape(tokens, group_count, NSTATE)
    readout_rows = out_matrix[0].astype(jnp.float32).reshape(tokens, group_count, NSTATE)
    output_gradient = grad_output[0].astype(jnp.float32).reshape(tokens, group_count, ratio, P_SIZE)
    running_state = jnp.cumsum(decays, axis=-1)
    totals = running_state[..., -1]
    local_state = jnp.einsum(
        "grs,sgn,sgrp->grnp",
        jnp.exp(totals[..., None] - running_state) * step_sizes,
        b_rows,
        x_rows,
        precision=PRECISION_LEVEL,
    )
    local_grad = jnp.einsum(
        "vad,dvm,dvah->vamh",
        jnp.exp(running_state),
        readout_rows,
        output_gradient,
        precision=PRECISION_LEVEL,
    )
    neutral = (jnp.zeros_like(totals), jnp.zeros_like(local_state))
    incoming = prefix((totals, local_state), "seq", join_pairs, neutral, False)[1]
    outgoing = prefix((totals, local_grad), "seq", join_pairs, neutral, True)[1]

    def local_map(x_arg, b_arg, c_arg, step_arg):
        return segment(x_arg, b_arg, c_arg, step_arg, -rates[..., None] * step_arg, incoming)

    forward_out, pullback = jax.vjp(local_map, x_rows, b_rows, readout_rows, step_sizes)
    grad_x, grad_b, grad_c, grad_step = pullback((output_gradient, outgoing))
    grad_pre = (
        jnp.transpose(grad_step.reshape(heads_here, tokens)) * jax.nn.sigmoid(preact)
    ).astype(jnp.bfloat16)
    partial_terms = lax.dot_general(
        grad_pre, step_weight, (((1,), (1,)), ((), ())), preferred_element_type=jnp.float32
    )
    grad_input = lax.psum_scatter(
        partial_terms.astype(jnp.bfloat16), "head", scatter_dimension=1, tiled=True
    )
    seq_part = lax.psum_scatter(
        lax.dot_general(
            whole_input, grad_pre, (((0,), (0,)), ((), ())), preferred_element_type=jnp.float32
        ).astype(jnp.bfloat16),
        "seq",
        scatter_dimension=0,
        tiled=True,
    ).astype(jnp.float32)
    grad_weight = lax.psum_scatter(seq_part, "dp", scatter_dimension=0, tiled=True)
    return (
        grad_x.reshape(tokens, heads_here * P_SIZE).astype(jnp.bfloat16)[None],
        grad_b.reshape(tokens, group_count * NSTATE).astype(jnp.bfloat16)[None],
        grad_c.reshape(tokens, group_count * NSTATE).astype(jnp.bfloat16)[None],
        grad_input[None],
        grad_weight,
    )


def solution(mesh):
    in_specs = (
        P("dp", "seq", "head"),
        P("dp", "seq", "head"),
        P("dp", "seq", "head"),
        P("dp", "seq", "head"),
        P("dp", "seq", "head"),
        P(None, "head"),
        P("head"),
        P("head"),
    )
    out_specs = (
        P("dp", "seq", "head"),
        P("dp", "seq", "head"),
        P("dp", "seq", "head"),
        P("dp", "seq", "head"),
        P(("seq", "dp"), "head"),
    )
    return jax.shard_map(body, mesh=mesh, in_specs=in_specs, out_specs=out_specs, check_vma=False)
```

profile of v0, /device:TPU:0, one launch (start us, length us, event | category | flops | bytes accessed | tf_op | source)
XLA Modules:
  0.0 142.0 jit_solution(7820624897420831480)
XLA Ops:
  7.3 0.7 all-gather.5.cloned.1.call-update
  8.0 1.1 copy.106
  9.2 1.2 copy.97
  10.4 0.7 iota_compare_fusion
  11.1 0.8 fusion.53
  11.9 17.2 %all-gather.5.cloned.1.call-done = bf16[1,128,4096]{2,1,0:T(8,128)(2,1)} async-done(((bf16[1,128,1024]{2,1,0:T(8,128)(2,1)}), bf16[1,128,4096]{2,1,0:T(8,128)(2,1)}) %all-gather.5.cloned.1.call-update) | async-done | bytes 1048592 | tf_op jit(solution)/shard_map/all_gather | solution.py:97
  29.1 1.6 %convolution_add_fusion.1 = f32[128,16]{1,0:T(8,128)S(1)} fusion(bf16[4096,16]{0,1:T(8,128)(2,1)S(1)} %copy-done, bf16[1,128,4096]{2,1,0:T(8,128)(2,1)} %all-gather.5.cloned.1.call-done, f32[16]{0:T(128)S(1)} %copy-done.23), kind=kOutput, calls=%fused_computation.25 | convolution fusion | flops 16779264 | bytes 1187904 | tf_op jit(solution)/shard_map/dot_general | solution.py:98
  30.9 0.3 reduce_window_sum.28
  31.3 0.7 fusion.46
  32.0 0.7 broadcast_subtract_fusion
  32.7 0.4 fusion.6
  33.1 9.1 %all-gather.2 = bf16[2,16,128,64]{2,3,1,0:T(8,128)(2,1)S(1)} all-gather(bf16[1,16,128,64]{2,3,1,0:T(8,128)(2,1)S(1)} %fusion.6), channel_id=4, replica_groups=mesh['seq'=2,'head'=4,'dp'=4] {'seq'}, dimensions={0}, use_global_device_ids=true | all-gather | bytes 786432 | tf_op jit(solution)/shard_map/all_gather | solution.py:21
  42.2 4.2 %all-gather = bf16[2,16,1]{1,2,0:T(2,128)(2,1)S(1)} all-gather(bf16[1,16,1]{1,2,0:T(2,128)(2,1)S(1)} %slice.10), channel_id=2, replica_groups=mesh['seq'=2,'head'=4,'dp'=4] {'seq'}, dimensions={0}, use_global_device_ids=true | all-gather | bytes 96 | tf_op jit(solution)/shard_map/all_gather | solution.py:21
  46.6 0.6 copy-done.24
  47.2 0.4 fusion.5
  47.6 7.5 %all-gather.1 = bf16[2,16,128,64]{2,3,1,0:T(8,128)(2,1)S(1)} all-gather(bf16[1,16,128,64]{2,3,1,0:T(8,128)(2,1)S(1)} %fusion.5), channel_id=3, replica_groups=mesh['seq'=2,'head'=4,'dp'=4] {'seq'}, dimensions={0}, use_global_device_ids=true | all-gather | bytes 786432 | tf_op jit(solution)/shard_map/all_gather | solution.py:21
  55.2 1.3 while.16
  55.2 0.3 copy.143
  55.5 0.7 exponential_bitcast_fusion.5
  56.5 2.0 %fusion.23 = (f32[128,16]{0,1:T(8,128)S(1)}, f32[128,16,64]{0,2,1:T(8,128)S(1)}) fusion(bf16[128,16,64]{0,2,1:T(8,128)(2,1)} %bitcast.245, bf16[1,128,128]{2,1,0:T(8,128)(2,1)} %param.14, f32[1,16,128,64]{3,2,1,0:T(8,128)S(1)} %get-tuple-element.283), kind=kOutput, calls=%fused_computation.48 | convolution fusion | flops 201717760 | bytes 1351680 | tf_op jit(solution)/shard_map/transpose(jvp())/while/body/eval_jaxpr/grs,sgn,sgrp->grnp/dot_general | solution.py:56
  58.5 0.8 multiply_reduce_fusion
  59.5 1.0 fusion.4
  60.5 0.7 copy.118
  61.2 0.7 copy.104
  61.9 2.5 %fusion.22 = (f32[16,128]{1,0:T(8,128)}, f32[16,128]{1,0:T(8,128)}, f32[16,128]{1,0:T(8,128)}, f32[128,128]{1,0:T(8,128)}) fusion(f32[16,128]{1,0:T(8,128)} %copy.104, f32[16,128]{1,0:T(8,128)S(1)} %bitcast.254, f32[128,128]{1,0:T(8,128)} %fusion.53, pred[128,128]{1,0:T(8,128)(4,1)} %iota_compare_fusion, bf16[16,64,128]{2,1,0:T(8,128)(2,1)S(1)} %bitcast.250, ...), kind=kOutput, calls=%fused_computation.47 | convolution fusion | flops 36939776 | bytes 712704 | tf_op jit(solution)/shard_map/transpose(jvp())/while/body/eval_jaxpr/idwz,zidx->widx/dot_general | solution.py:49
  64.4 1.4 copy.119
  65.8 1.4 copy.120
  67.3 0.7 bitcast_add_fusion
  68.0 1.6 %fusion.39 = (f32[1,16,128]{1,2,0:T(8,128)}, f32[128,16]{1,0:T(8,128)}) fusion(f32[128,16]{1,0:T(8,128)} %copy.118, f32[16,128]{0,1:T(8,128)} %copy.120, f32[16,128]{0,1:T(8,128)} %copy.119, f32[1,16,1]{1,2,0:T(1,128)S(1)} %bitcast_add_fusion, f32[1,16,128]{1,2,0:T(8,128)S(1)} %copy-done.8, f32[1,16,128]{1,2,0:T(8,128)S(1)} %copy.115, ...), kind=kLoop, calls=%fused_computation.67 | loop fusion | flops 30720 | bytes 73792 | tf_op jit(solution)/shard_map/transpose(jvp())/while/body/eval_jaxpr/add_any | solution.py:45
  69.6 0.9 copy.121
  70.5 1.3 reduce_window_sum.30
  71.7 0.7 broadcast_multiply_fusion
  72.5 0.7 copy.123
  73.2 1.4 copy.116
  74.6 0.9 fusion.36
  75.5 2.2 %fusion = bf16[4096,16]{0,1:T(8,128)(2,1)} fusion(bf16[128,16]{1,0:T(8,128)(2,1)S(1)} %fusion.36, bf16[1,128,4096]{2,1,0:T(8,128)(2,1)} %all-gather.5.cloned.1.call-done), kind=kOutput, calls=%fused_computation.8 | convolution fusion | flops 16842752 | bytes 1183744 | tf_op jit(solution)/shard_map/dot_general | solution.py:141
  77.8 9.5 %reduce-scatter.6.cloned.1.call-done = bf16[2048,16]{0,1:T(8,128)(2,1)} async-done(((bf16[4096,16]{0,1:T(8,128)(2,1)}), bf16[2048,16]{0,1:T(8,128)(2,1)}) %reduce-scatter.6.cloned.1.call-update) | async-done | bytes 65552 | tf_op jit(solution)/shard_map/reduce_scatter | solution.py:140
  87.2 1.5 %convert_element_type.178 = f32[2048,16]{0,1:T(8,128)} convert(bf16[2048,16]{0,1:T(8,128)(2,1)} %reduce-scatter.6.cloned.1.call-done) | non-fusion elementwise | flops 32768 | bytes 196608 | tf_op jit(solution)/shard_map/convert_element_type | solution.py:147
  89.0 1.4 convolution_convert_fusion
  90.5 0.3 convolution_bitcast_fusion.5
  90.8 1.0 fusion.10
  91.8 0.7 copy.125
  92.6 0.9 fusion.3
  93.5 0.9 copy.124
  94.3 1.8 %convolution_bitcast_fusion.3 = f32[128,128]{1,0:T(8,128)S(1)} fusion(f32[1,16,128,64]{3,2,1,0:T(8,128)S(1)} %get-tuple-element.284, bf16[128,1,16,64]{0,3,2,1:T(8,128)(2,1)S(1)} %bitcast.252, f32[128,16]{0,1:T(8,128)S(1)} %copy.110), kind=kOutput, calls=%fused_computation.20 | convolution fusion | flops 201588736 | bytes 860160 | tf_op jit(solution)/shard_map/transpose(jvp())/while/body/eval_jaxpr/tgn,grnp->tgrp/dot_general | solution.py:52
  96.2 0.8 fusion.11
  97.0 12.3 %reduce-scatter.8.cloned.1.call-done = f32[512,16]{0,1:T(8,128)} async-done(((f32[2048,16]{0,1:T(8,128)}), f32[512,16]{0,1:T(8,128)}) %reduce-scatter.8.cloned.1.call-update) | async-done | bytes 32784 | tf_op jit(solution)/shard_map/reduce_scatter | solution.py:148
  109.3 26.2 %reduce-scatter.4.cloned.1.call-done = bf16[128,1024]{1,0:T(8,128)(2,1)} async-done(((bf16[128,4096]{1,0:T(8,128)(2,1)}), bf16[128,1024]{1,0:T(8,128)(2,1)}) %reduce-scatter.4.cloned.1.call-update) | async-done | bytes 262160 | tf_op jit(solution)/shard_map/reduce_scatter | solution.py:137
  (73 shorter events, 1.6 us)
Async XLA Ops:
  7.2 21.9 %copy-start = (bf16[4096,16]{0,1:T(8,128)(2,1)S(1)}, bf16[4096,16]{0,1:T(8,128)(2,1)}, u32[]{:S(2)}) copy-start(bf16[4096,16]{0,1:T(8,128)(2,1)} %param.17) | copy-start | bytes 393220
  7.2 3.9 %copy-start.22 = (f32[16]{0:T(128)S(1)}, f32[16]{0:T(128)}, u32[]{:S(2)}) copy-start(f32[16]{0:T(128)} %param.19) | copy-start | bytes 196
  7.2 3.9 %copy-start.9 = (bf16[1,128,128]{2,1,0:T(8,128)(2,1)S(1)}, bf16[1,128,128]{2,1,0:T(8,128)(2,1)}, u32[]{:S(2)}) copy-start(bf16[1,128,128]{2,1,0:T(8,128)(2,1)} %param.14) | copy-start | bytes 98308
  7.2 3.9 %copy-start.11 = (bf16[1,128,128]{2,1,0:T(8,128)(2,1)S(1)}, bf16[1,128,128]{2,1,0:T(8,128)(2,1)}, u32[]{:S(2)}) copy-start(bf16[1,128,128]{2,1,0:T(8,128)(2,1)} %param.15) | copy-start | bytes 98308
  7.2 21.9 %copy-start.23 = (f32[16]{0:T(128)S(1)}, f32[16]{0:T(128)}, u32[]{:S(2)}) copy-start(f32[16]{0:T(128)} %param.18) | copy-start | bytes 196
  7.2 21.9 %all-gather.5.cloned.1.call-start = ((), (), s32[]{:S(2)}) async-start(), calls=%async_computation.3 | async-start | bytes 1310720 | tf_op jit(solution)/shard_map/all_gather | solution.py:97
  8.0 79.3 %reduce-scatter.6.cloned.1.call-start = ((), (), s32[]{:S(2)}) async-start(), calls=%async_computation.5 | async-start | bytes 196608 | tf_op jit(solution)/shard_map/reduce_scatter | solution.py:140
  9.1 23.6 %copy-start.1 = (bf16[1,128,1024]{1,2,0:T(8,128)(2,1)}, bf16[1,128,1024]{1,2,0:T(8,128)(2,1)S(1)}, u32[]{:S(2)}) copy-start(bf16[1,128,1024]{1,2,0:T(8,128)(2,1)S(1)} %copy.106) | copy-start | bytes 786436
  10.4 36.8 %copy-start.3 = (bf16[1,128,1024]{1,2,0:T(8,128)(2,1)}, bf16[1,128,1024]{1,2,0:T(8,128)(2,1)S(1)}, u32[]{:S(2)}) copy-start(bf16[1,128,1024]{1,2,0:T(8,128)(2,1)S(1)} %copy.97) | copy-start | bytes 786436
  11.1 19.7 %copy-start.21 = (f32[16]{0:T(128)}, f32[16]{0:T(128)S(1)}, u32[]{:S(2)}) copy-start(f32[16]{0:T(128)S(1)} %exponential_negate_fusion) | copy-start | bytes 196
  30.7 15.7 %copy-start.5 = (f32[128,16]{1,0:T(8,128)}, f32[128,16]{1,0:T(8,128)S(1)}, u32[]{:S(2)}) copy-start(f32[128,16]{1,0:T(8,128)S(1)} %convolution_add_fusion.1) | copy-start | bytes 24580
  31.3 1.4 %copy-start.7 = (f32[1,16,128]{1,2,0:T(8,128)}, f32[1,16,128]{1,2,0:T(8,128)S(1)}, u32[]{:S(2)}) copy-start(f32[1,16,128]{1,2,0:T(8,128)S(1)} %copy.94) | copy-start | bytes 24580
  46.6 0.6 copy-start.24
  58.4 0.9 copy-start.18
  58.5 1.0 copy-start.4
  58.5 1.0 copy-start.12
  59.3 2.0 %copy-start.14 = (f32[16,128]{0,1:T(8,128)S(1)}, f32[16,128]{0,1:T(8,128)}, u32[]{:S(2)}) copy-start(f32[16,128]{0,1:T(8,128)} %get-tuple-element.387) | copy-start | bytes 24580
  59.3 2.6 %copy-start.2 = (bf16[1,128,1024]{1,2,0:T(8,128)(2,1)S(1)}, bf16[1,128,1024]{1,2,0:T(8,128)(2,1)}, u32[]{:S(2)}) copy-start(bf16[1,128,1024]{1,2,0:T(8,128)(2,1)} %copy-done.1) | copy-start | bytes 786436
  61.9 5.3 %copy-start.6 = (f32[128,16]{1,0:T(8,128)S(1)}, f32[128,16]{1,0:T(8,128)}, u32[]{:S(2)}) copy-start(f32[128,16]{1,0:T(8,128)} %copy-done.5) | copy-start | bytes 24580
  61.9 5.4 %copy-start.8 = (f32[1,16,128]{1,2,0:T(8,128)S(1)}, f32[1,16,128]{1,2,0:T(8,128)}, u32[]{:S(2)}) copy-start(f32[1,16,128]{1,2,0:T(8,128)} %copy-done.7) | copy-start | bytes 24580
  77.7 31.6 %reduce-scatter.8.cloned.1.call-start = ((), (), s32[]{:S(2)}) async-start(), calls=%async_computation.6 | async-start | bytes 163840 | tf_op jit(solution)/shard_map/reduce_scatter | solution.py:148
  88.8 1.7 %copy-start.16 = (f32[128,16]{1,0:T(8,128)S(1)}, f32[128,16]{1,0:T(8,128)}, u32[]{:S(2)}) copy-start(f32[128,16]{1,0:T(8,128)} %get-tuple-element.385) | copy-start | bytes 24580
  88.8 1.7 %copy-start.13 = (bf16[1,128,128]{2,1,0:T(8,128)(2,1)S(1)}, bf16[1,128,128]{2,1,0:T(8,128)(2,1)}, u32[]{:S(2)}) copy-start(bf16[1,128,128]{2,1,0:T(8,128)(2,1)} %param.15) | copy-start | bytes 98308
  88.8 1.7 %copy-start.15 = (f32[128,128]{1,0:T(8,128)S(1)}, f32[128,128]{1,0:T(8,128)}, u32[]{:S(2)}) copy-start(f32[128,128]{1,0:T(8,128)} %get-tuple-element.363) | copy-start | bytes 196612
  88.8 46.7 %reduce-scatter.4.cloned.1.call-start = ((), (), s32[]{:S(2)}) async-start(), calls=%async_computation.4 | async-start | bytes 1310720 | tf_op jit(solution)/shard_map/reduce_scatter | solution.py:137
  90.4 2.1 %copy-start.17 = (f32[128,128]{1,0:T(8,128)S(1)}, f32[128,128]{1,0:T(8,128)}, u32[]{:S(2)}) copy-start(f32[128,128]{1,0:T(8,128)} %fusion.53) | copy-start | bytes 196612
  90.4 2.1 %copy-start.19 = (pred[128,128]{1,0:T(8,128)(4,1)S(1)}, pred[128,128]{1,0:T(8,128)(4,1)}, u32[]{:S(2)}) copy-start(pred[128,128]{1,0:T(8,128)(4,1)} %iota_compare_fusion) | copy-start | bytes 49156
  90.5 2.1 %copy-start.20 = (f32[16,128]{1,0:T(8,128)S(1)}, f32[16,128]{1,0:T(8,128)}, u32[]{:S(2)}) copy-start(f32[16,128]{1,0:T(8,128)} %copy.104) | copy-start | bytes 24580
  93.5 2.7 %copy-start.10 = (bf16[1,128,128]{2,1,0:T(8,128)(2,1)S(1)}, bf16[1,128,128]{2,1,0:T(8,128)(2,1)}, u32[]{:S(2)}) copy-start(bf16[1,128,128]{2,1,0:T(8,128)(2,1)} %param.14) | copy-start | bytes 98308
Sparse Core Ops, SparseCore 0:
  9.6 19.4 all-gather.4
  77.9 9.3 reduce-scatter.5
  90.1 19.1 reduce-scatter.7
  112.4 23.0 reduce-scatter.3
where the time goes:
time: 143 us; the launch traced here: 142 us
  waiting for transfers between devices  65.9 us (46%)
  blocking collectives  20.8 us (15%)
  matrix products  17 us (12%)
  between operations  14.1 us (10%)
  local copies, waits for them, and re-layouts  12.9 us (9%)
  other arithmetic  10.8 us (8%)
    reduce_scatter x1, waiting for transfers between devices, body(): lax.psum_scatter(partial_terms.astype(jnp.bfloat16), 'head', scatter_dime...  26.2 us
    all_gather x3, blocking collectives, prefix(): lax.all_gather(a.astype(kind), axis)  20.8 us
    all_gather x1, waiting for transfers between devices, body(): whole_input = lax.all_gather(layer_input, 'head', axis=2, tiled=True)[0]  17.2 us
    reduce_scatter x1, waiting for transfers between devices, body(): lax.psum_scatter(seq_part, 'dp', scatter_dimension=0, tiled=True)  12.3 us
    reduce_scatter x1, waiting for transfers between devices, body(): lax.psum_scatter(lax.dot_general(whole_input, grad_pre, (((0,), (0,)), ((...  9.46 us
    unnamed x54, local copies, waits for them, and re-layouts  4.59 us
    dot_general x2, matrix products, block_step(): jnp.einsum('idwz,zidx->widx', weight_values, input_block, precision=PRECI...  3.37 us
    dot_general x2, matrix products, block_step(): jnp.einsum('grs,sgn,sgrp->grnp', inflow, b_block, input_block, precision=...  3.01 us
  transfers between devices with their start and end apart: 4, of which 4 were waited for; matrix products, arithmetic and copies ran while one was open for 8% of the time, Pallas kernels for 0%

commit v1 on v0

--- a/solution.py
+++ b/solution.py
@@ -1,6 +1,10 @@
+import functools
+
 import jax
 import jax.numpy as jnp
 from jax import lax
+from jax.experimental import pallas as pl
+from jax.experimental.pallas import tpu as pltpu
 from jax.sharding import PartitionSpec as P
 
 H = 64
@@ -155,6 +159,412 @@
     )
 
 
+MESH = pl.DeviceIdType.MESH
+NT = (((1,), (1,)), ((), ()))
+NN = (((1,), (0,)), ((), ()))
+TN = (((0,), (0,)), ((), ()))
+
+
+def mm(a, b, dims):
+    return lax.dot_general(a, b, dims, preferred_element_type=jnp.float32)
+
+
+def exact_mm(a, b):
+    return lax.dot_general(
+        a, b, NN, precision=lax.Precision.HIGHEST, preferred_element_type=jnp.float32
+    )
+
+
+def two_parts(v):
+    high = v.astype(jnp.bfloat16)
+    low = (v - high.astype(jnp.float32)).astype(jnp.bfloat16)
+    return high, low
+
+
+def softplus(v):
+    return jnp.maximum(v, 0.0) + jnp.log1p(jnp.exp(-jnp.abs(v)))
+
+
+def mixer_kernel(
+    sizes,
+    layer_hbm, x_hbm, b_hbm, c_hbm, gy_hbm, w_hbm, bias_ref, rate_ref,
+    gx_ref, gb_ref, gc_ref, gin_ref, gw_ref,
+    layer, xg, bc, far_xg, far_bc, w_all, part, part_far, mt, ke, qcol, gp_all, gw_send, gw_recv,
+    load_sem, w_send, w_recv, raw_send, raw_recv, p_send, p_recv, g_send, g_recv, d_send, d_recv,
+):
+    n_seq, n_head, n_dp, heads, p_size = sizes
+    tokens, feats = layer.shape
+    me_s, me_h, me_d = lax.axis_index("seq"), lax.axis_index("head"), lax.axis_index("dp")
+    far_s = 1 - me_s
+    rows_out = gw_ref.shape[1]
+    cuts = feats // rows_out
+    share = n_seq * n_dp
+
+    def head_at(k):
+        return lax.rem(me_h + k, n_head)
+
+    def place(s, h, d):
+        return {"seq": s, "head": h, "dp": d}
+
+    loads = [
+        pltpu.make_async_copy(x_hbm, xg.at[0], load_sem.at[0]),
+        pltpu.make_async_copy(gy_hbm, xg.at[1], load_sem.at[1]),
+        pltpu.make_async_copy(b_hbm, bc.at[0], load_sem.at[2]),
+        pltpu.make_async_copy(c_hbm, bc.at[1], load_sem.at[3]),
+        pltpu.make_async_copy(layer_hbm, layer, load_sem.at[4]),
+        pltpu.make_async_copy(
+            w_hbm.at[:, pl.ds(pl.multiple_of(me_h * feats, feats), feats)],
+            w_all.at[pl.ds(pl.multiple_of(me_h * heads, heads), heads)],
+            load_sem.at[5],
+        ),
+    ]
+    for load in loads:
+        load.start()
+
+    barrier = pltpu.get_barrier_semaphore()
+    my_row = me_s * n_dp + me_d
+    source_h = my_row // cuts
+    for k in range(n_head):
+        if k:
+            pl.semaphore_signal(
+                barrier, inc=1, device_id=place(me_s, head_at(k), me_d), device_id_type=MESH
+            )
+        pl.semaphore_signal(
+            barrier, inc=1, device_id=place(far_s, head_at(k), me_d), device_id_type=MESH
+        )
+    mine = source_h == me_h
+    for k in range(share):
+        spot = lax.rem(my_row + k, share)
+
+        def greet():
+            pl.semaphore_signal(
+                barrier,
+                inc=1,
+                device_id=place(spot // n_dp, source_h, lax.rem(spot, n_dp)),
+                device_id_type=MESH,
+            )
+
+        if k:
+            greet()
+        else:
+            pl.when(jnp.logical_not(mine))(greet)
+    pl.semaphore_wait(barrier, 2 * n_head - 1 + share - jnp.where(mine, 1, 0))
+
+    w_copies = []
+    for k in range(1, n_head):
+        to = head_at(k)
+        copy = pltpu.make_async_remote_copy(
+            src_ref=w_hbm.at[:, pl.ds(pl.multiple_of(to * feats, feats), feats)],
+            dst_ref=w_all.at[pl.ds(pl.multiple_of(me_h * heads, heads), heads)],
+            send_sem=w_send.at[k - 1],
+            recv_sem=w_recv.at[k - 1],
+            device_id=place(me_s, to, me_d),
+            device_id_type=MESH,
+        )
+        copy.start()
+        w_copies.append(copy)
+
+    for load in loads[:4]:
+        load.wait()
+    raw_copies = []
+    for at, (near, far) in enumerate(((bc, far_bc), (xg, far_xg))):
+        copy = pltpu.make_async_remote_copy(
+            src_ref=near.at[me_s],
+            dst_ref=far,
+            send_sem=raw_send.at[at],
+            recv_sem=raw_recv.at[at],
+            device_id=place(far_s, me_h, me_d),
+            device_id_type=MESH,
+        )
+        copy.start()
+        raw_copies.append(copy)
+
+    pair = 2 * p_size
+    left = lax.broadcasted_iota(jnp.int32, (tokens, pair), 1) < p_size
+    kt = mm(bc[0], bc[1], NT)
+    zero_pair = jnp.zeros((tokens, pair), jnp.bfloat16)
+    for j in range(heads // 2):
+        lanes = slice(j * pair, (j + 1) * pair)
+        x_pair, gy_pair = xg[0, :, lanes], xg[1, :, lanes]
+        mt[2 * j] = mm(jnp.where(left, x_pair, zero_pair), gy_pair, NT)
+        mt[2 * j + 1] = mm(jnp.where(left, zero_pair, x_pair), gy_pair, NT)
+
+    loads[4].wait()
+    loads[5].wait()
+    for copy in w_copies:
+        copy.wait_recv()
+    part[...] = mm(w_all[...], layer[...], NT)
+    part_copies = []
+    for k in range(n_head):
+        to = head_at(k)
+        for hop in range(2):
+            if k == 0 and hop == 0:
+                continue
+            at = 2 * k + hop - 1
+            copy = pltpu.make_async_remote_copy(
+                src_ref=part.at[pl.ds(pl.multiple_of(to * heads, heads), heads)],
+                dst_ref=part_far.at[at],
+                send_sem=p_send.at[at],
+                recv_sem=p_recv.at[at],
+                device_id=place(far_s if hop else me_s, to, me_d),
+                device_id_type=MESH,
+            )
+            copy.start()
+            part_copies.append(copy)
+
+    upper = (
+        lax.broadcasted_iota(jnp.int32, (tokens, tokens), 0)
+        <= lax.broadcasted_iota(jnp.int32, (tokens, tokens), 1)
+    )
+    summing = upper.astype(jnp.float32)
+    square = lax.broadcasted_iota(jnp.int32, (heads, heads), 0) == lax.broadcasted_iota(
+        jnp.int32, (heads, heads), 1
+    )
+
+    def column(row):
+        return jnp.sum(jnp.where(square, row, 0.0), axis=1, keepdims=True)
+
+    bias = column(bias_ref[...])
+    rate = jnp.exp(column(rate_ref[...]))
+    spread_rows = lax.rem(lax.broadcasted_iota(jnp.int32, (2 * heads, heads * p_size), 0), heads)
+    spread_at = lax.broadcasted_iota(jnp.int32, (2 * heads, heads * p_size), 1) // p_size
+    spread = jnp.where(spread_rows == spread_at, 1.0, 0.0).astype(jnp.bfloat16)
+
+    def widen(v):
+        high, low = two_parts(v)
+        return mm(jnp.concatenate([high, low], axis=0), spread, TN)
+
+    for k in range(1, n_head):
+        part_copies[2 * k - 1].wait_recv()
+    preact = part[pl.ds(pl.multiple_of(me_h * heads, heads), heads), :] + bias
+    for k in range(1, n_head):
+        preact = preact + part_far[2 * k - 1]
+    dt = softplus(preact)
+    cum = exact_mm(-rate * dt, summing)
+    total = cum[:, tokens - 1 :]
+    cum_col = jnp.transpose(cum)
+    dt_col = jnp.transpose(dt)
+    dkt = jnp.zeros((tokens, tokens), jnp.float32)
+    r_rows = []
+    for h in range(heads):
+        gap = cum[h : h + 1, :] - cum_col[:, h : h + 1]
+        span = jnp.exp(jnp.where(upper, gap, -1e30))
+        ke[h] = (kt * span).astype(jnp.bfloat16)
+        step_here = dt_col[:, h : h + 1]
+        f = mt[h] * span
+        dkt = dkt + f * step_here
+        prod = f * kt
+        qcol[:, h : h + 1] = jnp.sum(prod, axis=1, keepdims=True)
+        r_rows.append(jnp.sum(prod * step_here, axis=0, keepdims=True))
+    r = jnp.concatenate(r_rows, axis=0)
+    q = jnp.transpose(qcol[...])[:heads]
+
+    first = me_s == 0
+    for k in range(n_head):
+        part_copies[2 * k].wait_recv()
+    far_pre = bias
+    for k in range(n_head):
+        far_pre = far_pre + part_far[2 * k]
+    far_dt = softplus(far_pre)
+    far_cum = exact_mm(-rate * far_dt, summing)
+    far_total = far_cum[:, tokens - 1 :]
+    from_start = jnp.exp(cum)
+    to_end = jnp.exp(total - cum)
+    far_scale = jnp.where(first, jnp.exp(far_cum), jnp.exp(far_total - far_cum) * far_dt)
+    near_scale = jnp.where(first, to_end * dt, from_start)
+    far_wide = widen(far_scale)
+    near_wide = widen(near_scale)
+    for copy in raw_copies:
+        copy.wait_recv()
+    state = mm(
+        far_bc[...], (far_xg[...].astype(jnp.float32) * far_wide).astype(jnp.bfloat16), TN
+    ).astype(jnp.bfloat16)
+    carried = mm(bc[me_s], state, NN)
+    near = xg[me_s].astype(jnp.float32)
+    high, low = two_parts(near * carried)
+    w = mm(spread[:heads], high, NT) + mm(spread[:heads], low, NT)
+
+    v = to_end * w
+    q = jnp.where(first, q + v, q)
+    da = r - dt * q + jnp.where(first, 0.0, from_start * w)
+    at_end = jnp.where(first, jnp.sum(dt * v, axis=1, keepdims=True), 0.0)
+    lower = (
+        lax.broadcasted_iota(jnp.int32, (tokens, tokens), 0)
+        >= lax.broadcasted_iota(jnp.int32, (tokens, tokens), 1)
+    ).astype(jnp.float32)
+    grad_step = q - rate * (exact_mm(da, lower) + at_end)
+    my_rows = pl.ds(pl.multiple_of(me_h * heads, heads), heads)
+    gp_all[my_rows, :] = (grad_step * jax.nn.sigmoid(preact)).astype(jnp.bfloat16)
+    gp_copies = []
+    for k in range(1, n_head):
+        copy = pltpu.make_async_remote_copy(
+            src_ref=gp_all.at[my_rows],
+            dst_ref=gp_all.at[my_rows],
+            send_sem=g_send.at[k - 1],
+            recv_sem=g_recv.at[k - 1],
+            device_id=place(me_s, head_at(k), me_d),
+            device_id_type=MESH,
+        )
+        copy.start()
+        gp_copies.append(copy)
+
+    dt_wide = widen(dt)
+    flag = jnp.where(first, 1.0, 0.0)
+    for j in range(heads // 2):
+        lanes = slice(j * pair, (j + 1) * pair)
+        gy_pair = xg[1, :, lanes]
+        inner = jnp.where(left, mm(ke[2 * j], gy_pair, NN), mm(ke[2 * j + 1], gy_pair, NN))
+        gx_ref[:, lanes] = (
+            inner * dt_wide[:, lanes] + flag * near_wide[:, lanes] * carried[:, lanes]
+        ).astype(jnp.bfloat16)
+    extra = mm((near * near_wide).astype(jnp.bfloat16), state, NT)
+    dk = dkt.astype(jnp.bfloat16)
+    gb_ref[...] = (mm(dk, bc[1], NN) + flag * extra).astype(jnp.bfloat16)
+    gc_ref[...] = (mm(dk, bc[0], TN) + (1.0 - flag) * extra).astype(jnp.bfloat16)
+
+    for copy in gp_copies:
+        copy.wait_recv()
+    gw_send[...] = mm(gp_all[...], layer[...], NN).astype(jnp.bfloat16)
+    gw_copies = []
+    for cut in range(cuts):
+        row = me_h * cuts + cut
+        to_s, to_d = row // n_dp, lax.rem(row, n_dp)
+        for k in range(n_head):
+            to = head_at(k)
+            at = cut * n_head + k
+            block = gw_send.at[
+                pl.ds(pl.multiple_of(to * heads, heads), heads),
+                cut * rows_out : (cut + 1) * rows_out,
+            ]
+            copy = pltpu.make_async_remote_copy(
+                src_ref=block,
+                dst_ref=gw_recv.at[my_row],
+                send_sem=d_send.at[at],
+                recv_sem=d_recv.at[my_row],
+                device_id=place(to_s, to, to_d),
+                device_id_type=MESH,
+            )
+            if k:
+                copy.start()
+                gw_copies.append((copy, None))
+            else:
+                away = row != my_row
+                pl.when(away)(copy.start)
+                gw_copies.append((copy, away))
+
+                @pl.when(jnp.logical_not(away))
+                def _():
+                    gw_recv[my_row] = block[...]
+
+    gin = jnp.zeros((tokens, feats), jnp.float32)
+    for j in range(n_head):
+        rows = slice(j * heads, (j + 1) * heads)
+        term = mm(gp_all[rows, :], w_all[rows, :], TN)
+        gin = gin + term.astype(jnp.bfloat16).astype(jnp.float32)
+    gin_ref[...] = gin.astype(jnp.bfloat16)
+
+    def arrived(k):
+        spot = lax.rem(my_row + k, share)
+        return pltpu.make_async_remote_copy(
+            src_ref=gw_recv.at[spot],
+            dst_ref=gw_recv.at[spot],
+            send_sem=d_send.at[0],
+            recv_sem=d_recv.at[spot],
+            device_id=place(far_s, me_h, me_d),
+            device_id_type=MESH,
+        )
+
+    for k in range(1, share):
+        arrived(k).wait_recv()
+    pl.when(jnp.logical_not(mine))(arrived(0).wait_recv)
+    gw = gw_recv[0].astype(jnp.float32)
+    for k in range(1, share):
+        gw = gw + gw_recv[k].astype(jnp.float32)
+    gw_ref[...] = gw
+
+    for copy in w_copies + raw_copies + part_copies + gp_copies:
+        copy.wait_send()
+    for copy, away in gw_copies:
+        if away is None:
+            copy.wait_send()
+        else:
+            pl.when(away)(copy.wait_send)
+
+
+def fused_body(
+    mesh, layer_input, head_input, in_matrix, out_matrix, grad_output, step_weight, step_bias, decay_log
+):
+    n_seq, n_head, n_dp = (mesh.shape[a] for a in ("seq", "head", "dp"))
+    tokens, feats = layer_input.shape[1:]
+    width = head_input.shape[2]
+    state_size = in_matrix.shape[2]
+    heads = step_bias.shape[0]
+    rows_out = step_weight.shape[0] // (n_seq * n_dp)
+    share = n_seq * n_dp
+    b16, f32 = jnp.bfloat16, jnp.float32
+    dma = pltpu.SemaphoreType.DMA
+    hbm = pl.BlockSpec(memory_space=pl.ANY)
+    vmem = pl.BlockSpec(memory_space=pltpu.VMEM)
+    gx, gb, gc, gin, gw = pl.pallas_call(
+        functools.partial(mixer_kernel, (n_seq, n_head, n_dp, heads, width // heads)),
+        out_shape=(
+            jax.ShapeDtypeStruct((tokens, width), b16),
+            jax.ShapeDtypeStruct((tokens, state_size), b16),
+            jax.ShapeDtypeStruct((tokens, state_size), b16),
+            jax.ShapeDtypeStruct((tokens, feats), b16),
+            jax.ShapeDtypeStruct((heads, rows_out), f32),
+        ),
+        in_specs=[hbm] * 6 + [vmem] * 2,
+        out_specs=[vmem] * 5,
+        scratch_shapes=[
+            pltpu.VMEM((tokens, feats), b16),
+            pltpu.VMEM((2, tokens, width), b16),
+            pltpu.VMEM((2, tokens, state_size), b16),
+            pltpu.VMEM((tokens, width), b16),
+            pltpu.VMEM((tokens, state_size), b16),
+            pltpu.VMEM((n_head * heads, feats), b16),
+            pltpu.VMEM((n_head * heads, tokens), f32),
+            pltpu.VMEM((2 * n_head - 1, heads, tokens), f32),
+            pltpu.VMEM((heads, tokens, tokens), f32),
+            pltpu.VMEM((heads, tokens, tokens), b16),
+            pltpu.VMEM((tokens, tokens), f32),
+            pltpu.VMEM((n_head * heads, tokens), b16),
+            pltpu.VMEM((n_head * heads, feats), b16),
+            pltpu.VMEM((share, heads, rows_out), b16),
+            dma((6,)),
+            dma((n_head - 1,)),
+            dma((n_head - 1,)),
+            dma((2,)),
+            dma((2,)),
+            dma((2 * n_head - 1,)),
+            dma((2 * n_head - 1,)),
+            dma((n_head - 1,)),
+            dma((n_head - 1,)),
+            dma((share,)),
+            dma((share,)),
+        ],
+        compiler_params=pltpu.CompilerParams(
+            collective_id=0, has_side_effects=True, vmem_limit_bytes=32 * 1024 * 1024
+        ),
+        name="mixer",
+    )(
+        layer_input[0], head_input[0], in_matrix[0], out_matrix[0], grad_output[0],
+        jnp.transpose(step_weight), step_bias[None], decay_log[None],
+    )
+    return gx[None], gb[None], gc[None], gin[None], jnp.transpose(gw)
+
+
+def fits(mesh, args):
+    n_seq, n_head, n_dp = (mesh.shape[a] for a in ("seq", "head", "dp"))
+    tokens = args[0].shape[1] // n_seq
+    return (
+        n_seq == 2
+        and n_head == G
+        and tokens == BLOCK
+        and (n_seq * n_dp) % n_head == 0
+    )
+
+
 def solution(mesh):
     in_specs = (
         P("dp", "seq", "head"),
@@ -173,4 +583,11 @@
         P("dp", "seq", "head"),
         P(("seq", "dp"), "head"),
     )
-    return jax.shard_map(body, mesh=mesh, in_specs=in_specs, out_specs=out_specs, check_vma=False)
+
+    def run(*args):
+        here = functools.partial(fused_body, mesh) if fits(mesh, args) else body
+        return jax.shard_map(
+            here, mesh=mesh, in_specs=in_specs, out_specs=out_specs, check_vma=False
+        )(*args)
+
+    return run

time: 143 us -> 34.6 us (0.24)
  waiting for transfers between devices: 65.9 us -> 0 us
  Pallas kernels: 0 us -> 24.3 us
  blocking collectives: 20.8 us -> 0 us
  matrix products: 17 us -> 0 us
  between operations: 14.1 us -> 0.67 us
  other arithmetic: 10.8 us -> 0 us
  local copies, waits for them, and re-layouts: 12.9 us -> 9.17 us
    reduce_scatter x3 -> x0, waiting for transfers between devices: 48 us -> none  [the longest x1 26.2 us: body(): lax.psum_scatter(partial_terms.astype(jnp.bfloat16), 'head', scatter_dime...]
    pallas_call x0 -> x1, Pallas kernels: none -> 24.3 us  [fused_body(): pl.pallas_call(functools.partial(mixer_kernel, (n_seq, n_head, n_dp, head...]
    all_gather x3 -> x0, blocking collectives: 20.8 us -> none  [prefix(): lax.all_gather(a.astype(kind), axis)]
    all_gather x1 -> x0, waiting for transfers between devices: 17.2 us -> none  [body(): whole_input = lax.all_gather(layer_input, 'head', axis=2, tiled=True)[0]]
    dot_general x14 -> x0, matrix products: 17 us -> none  [the longest x2 3.37 us: block_step(): jnp.einsum('idwz,zidx->widx', weight_values, input_block, precision=PRECI...]
    reduce_sum x4 -> x0, local copies, waits for them, and re-layouts: 4.98 us -> none  [the longest x2 2.83 us: block_step(): cumulated[..., :, None] - cumulated[..., None, :]]
    unnamed x54 -> x21, local copies, waits for them, and re-layouts: 4.59 us -> 9.17 us
    convert_element_type x2 -> x0, other arithmetic: 2.41 us -> none  [the longest x1 1.5 us: body(): seq_part = lax.psum_scatter(lax.dot_general(whole_input, grad_pre, (((0,)...]
  transfers between devices with their start and end apart: 4 -> 0, of which waited for: 4 -> 0; matrix products, arithmetic and copies ran while one was open for 8% -> 0% of each run, Pallas kernels for 0% -> 0%
where the time goes in v1:
time: 34.6 us; the launch traced here: 34.2 us
  Pallas kernels  24.3 us (70%)
  local copies, waits for them, and re-layouts  9.17 us (27%)
  between operations  0.67 us (2%)
    pallas_call x1, Pallas kernels, fused_body(): pl.pallas_call(functools.partial(mixer_kernel, (n_seq, n_head, n_dp, head...  24.3 us
    unnamed x21, local copies, waits for them, and re-layouts  9.17 us

profile of v1, /device:TPU:0, one launch (start us, length us, event | category | flops | bytes accessed | tf_op | source)
XLA Modules:
  0.0 34.2 jit_solution(2706375401060297247)
XLA Ops:
  0.6 0.0 copy-start.6
  0.6 0.0 copy-start.7
  0.7 0.6 %copy-done.6 = f32[16]{0:T(128)S(1)} copy-done((f32[16]{0:T(128)S(1)}, f32[16]{0:T(128)}, u32[]{:S(2)}) %copy-start.6) | copy-done | bytes 88
  1.3 0.0 copy-done.7
  1.3 0.0 copy-start
  1.3 0.9 %copy-done = bf16[1,128,1024]{2,1,0:T(8,128)(2,1)S(1)} copy-done((bf16[1,128,1024]{2,1,0:T(8,128)(2,1)S(1)}, bf16[1,128,1024]{2,1,0:T(8,128)(2,1)}, u32[]{:S(2)}) %copy-start) | copy-done | bytes 262168
  2.3 0.0 copy-start.1
  2.3 0.9 %copy-done.1 = bf16[1,128,1024]{2,1,0:T(8,128)(2,1)S(1)} copy-done((bf16[1,128,1024]{2,1,0:T(8,128)(2,1)S(1)}, bf16[1,128,1024]{2,1,0:T(8,128)(2,1)}, u32[]{:S(2)}) %copy-start.1) | copy-done | bytes 262168
  3.2 0.0 copy-start.2
  3.2 0.9 %copy-done.2 = bf16[1,128,1024]{2,1,0:T(8,128)(2,1)S(1)} copy-done((bf16[1,128,1024]{2,1,0:T(8,128)(2,1)S(1)}, bf16[1,128,1024]{2,1,0:T(8,128)(2,1)}, u32[]{:S(2)}) %copy-start.2) | copy-done | bytes 262168
  4.2 0.0 copy-start.3
  4.2 0.9 %copy-done.3 = bf16[4096,16]{0,1:T(8,128)(2,1)S(1)} copy-done((bf16[4096,16]{0,1:T(8,128)(2,1)S(1)}, bf16[4096,16]{0,1:T(8,128)(2,1)}, u32[]{:S(2)}) %copy-start.3) | copy-done | bytes 131096
  5.1 0.0 copy-start.4
  5.1 0.8 %copy-done.4 = bf16[1,128,128]{2,1,0:T(8,128)(2,1)S(1)} copy-done((bf16[1,128,128]{2,1,0:T(8,128)(2,1)S(1)}, bf16[1,128,128]{2,1,0:T(8,128)(2,1)}, u32[]{:S(2)}) %copy-start.4) | copy-done | bytes 32792
  5.8 0.0 copy-start.5
  5.8 0.8 %copy-done.5 = bf16[1,128,128]{2,1,0:T(8,128)(2,1)S(1)} copy-done((bf16[1,128,128]{2,1,0:T(8,128)(2,1)S(1)}, bf16[1,128,128]{2,1,0:T(8,128)(2,1)}, u32[]{:S(2)}) %copy-start.5) | copy-done | bytes 32792
  6.6 24.3 %mixer.1 = (bf16[128,1024]{1,0:T(8,128)(2,1)S(1)}, bf16[128,128]{1,0:T(8,128)(2,1)S(1)}, bf16[128,128]{1,0:T(8,128)(2,1)S(1)}, bf16[128,1024]{1,0:T(8,128)(2,1)S(1)}, f32[16,512]{1,0:T(8,128)S(1)}) custom-call(bf16[128,1024]{1,0:T(8,128)(2,1)S(1)} %bitcast.13, bf16[128,1024]{1,0:T(8,128)(2,1)S(1)} %bitcast.14, bf16[128,128]{1,0:T(8,128)(2,1)S(1)} %bitcast.19, ...), custom_call_target="tpu_custom_call" | custom-call | tf_op jit(solution)/shard_map/mixer/pallas_call | solution.py:508
  30.9 0.7 %copy.18 = bf16[1,128,1024]{2,1,0:T(8,128)(2,1)} copy(bf16[1,128,1024]{2,1,0:T(8,128)(2,1)S(1)} %bitcast.17) | data formatting | bytes 524288
  31.6 0.6 %copy.19 = bf16[1,128,128]{2,1,0:T(8,128)(2,1)} copy(bf16[1,128,128]{2,1,0:T(8,128)(2,1)S(1)} %bitcast.23) | data formatting | bytes 65536
  32.2 0.6 %copy.20 = bf16[1,128,128]{2,1,0:T(8,128)(2,1)} copy(bf16[1,128,128]{2,1,0:T(8,128)(2,1)S(1)} %bitcast.22) | data formatting | bytes 65536
  32.9 0.7 %copy.21 = bf16[1,128,1024]{2,1,0:T(8,128)(2,1)} copy(bf16[1,128,1024]{2,1,0:T(8,128)(2,1)S(1)} %bitcast.16) | data formatting | bytes 524288
  33.6 0.6 %copy.22 = f32[512,16]{0,1:T(8,128)} copy(f32[512,16]{0,1:T(8,128)S(1)} %bitcast.21) | data formatting | bytes 65536
Async XLA Ops:
  0.6 0.7 %copy-start.6 = (f32[16]{0:T(128)S(1)}, f32[16]{0:T(128)}, u32[]{:S(2)}) copy-start(f32[16]{0:T(128)} %param.14) | copy-start | bytes 196
  0.6 0.7 %copy-start.7 = (f32[16]{0:T(128)S(1)}, f32[16]{0:T(128)}, u32[]{:S(2)}) copy-start(f32[16]{0:T(128)} %param.15) | copy-start | bytes 196
  1.3 0.9 %copy-start = (bf16[1,128,1024]{2,1,0:T(8,128)(2,1)S(1)}, bf16[1,128,1024]{2,1,0:T(8,128)(2,1)}, u32[]{:S(2)}) copy-start(bf16[1,128,1024]{2,1,0:T(8,128)(2,1)} %param.8) | copy-start | bytes 786436
  2.3 0.9 %copy-start.1 = (bf16[1,128,1024]{2,1,0:T(8,128)(2,1)S(1)}, bf16[1,128,1024]{2,1,0:T(8,128)(2,1)}, u32[]{:S(2)}) copy-start(bf16[1,128,1024]{2,1,0:T(8,128)(2,1)} %param.9) | copy-start | bytes 786436
  3.2 0.9 %copy-start.2 = (bf16[1,128,1024]{2,1,0:T(8,128)(2,1)S(1)}, bf16[1,128,1024]{2,1,0:T(8,128)(2,1)}, u32[]{:S(2)}) copy-start(bf16[1,128,1024]{2,1,0:T(8,128)(2,1)} %param.12) | copy-start | bytes 786436
  4.2 0.9 %copy-start.3 = (bf16[4096,16]{0,1:T(8,128)(2,1)S(1)}, bf16[4096,16]{0,1:T(8,128)(2,1)}, u32[]{:S(2)}) copy-start(bf16[4096,16]{0,1:T(8,128)(2,1)} %param.13) | copy-start | bytes 393220
  5.1 0.8 %copy-start.4 = (bf16[1,128,128]{2,1,0:T(8,128)(2,1)S(1)}, bf16[1,128,128]{2,1,0:T(8,128)(2,1)}, u32[]{:S(2)}) copy-start(bf16[1,128,128]{2,1,0:T(8,128)(2,1)} %param.10) | copy-start | bytes 98308
  5.8 0.8 %copy-start.5 = (bf16[1,128,128]{2,1,0:T(8,128)(2,1)S(1)}, bf16[1,128,128]{2,1,0:T(8,128)(2,1)}, u32[]{:S(2)}) copy-start(bf16[1,128,128]{2,1,0:T(8,128)(2,1)} %param.11) | copy-start | bytes 98308

commit v2 on v1

--- a/solution.py
+++ b/solution.py
@@ -160,6 +160,7 @@
 
 
 MESH = pl.DeviceIdType.MESH
+CHUNKS = 4
 NT = (((1,), (1,)), ((), ()))
 NN = (((1,), (0,)), ((), ()))
 TN = (((0,), (0,)), ((), ()))
@@ -187,9 +188,10 @@
 
 def mixer_kernel(
     sizes,
-    layer_hbm, x_hbm, b_hbm, c_hbm, gy_hbm, w_hbm, bias_ref, rate_ref,
-    gx_ref, gb_ref, gc_ref, gin_ref, gw_ref,
-    layer, xg, bc, far_xg, far_bc, w_all, part, part_far, mt, ke, qcol, gp_all, gw_send, gw_recv,
+    layer_hbm, x_hbm, b_hbm, c_hbm, gy_hbm, w_hbm, bias_hbm, rate_hbm,
+    gx_hbm, gb_hbm, gc_hbm, gin_hbm, gw_hbm,
+    gx_ref, gb_ref, gc_ref, gin_ref, gw_ref, out_sem,
+    bias_ref, rate_ref, layer, xg, bc, far_xg, far_bc, w_all, part, part_far, mt, ke, qcol, gp_all, gw_send, gw_recv,
     load_sem, w_send, w_recv, raw_send, raw_recv, p_send, p_recv, g_send, g_recv, d_send, d_recv,
 ):
     n_seq, n_head, n_dp, heads, p_size = sizes
@@ -205,6 +207,19 @@
 
     def place(s, h, d):
         return {"seq": s, "head": h, "dp": d}
+
+    stores = [
+        pltpu.make_async_copy(src, dst, out_sem.at[at])
+        for at, (src, dst) in enumerate(
+            (
+                (gx_ref, gx_hbm),
+                (gb_ref, gb_hbm),
+                (gc_ref, gc_hbm),
+                (gin_ref, gin_hbm),
+                (gw_ref, gw_hbm),
+            )
+        )
+    ]
 
     loads = [
         pltpu.make_async_copy(x_hbm, xg.at[0], load_sem.at[0]),
@@ -217,6 +232,8 @@
             w_all.at[pl.ds(pl.multiple_of(me_h * heads, heads), heads)],
             load_sem.at[5],
         ),
+        pltpu.make_async_copy(bias_hbm, bias_ref, load_sem.at[6]),
+        pltpu.make_async_copy(rate_hbm, rate_ref, load_sem.at[7]),
     ]
     for load in loads:
         load.start()
@@ -267,10 +284,14 @@
     for load in loads[:4]:
         load.wait()
     raw_copies = []
-    for at, (near, far) in enumerate(((bc, far_bc), (xg, far_xg))):
+    width = far_xg.shape[1] // CHUNKS
+    chunks = [slice(c * width, (c + 1) * width) for c in range(CHUNKS)]
+    near_refs = [bc.at[me_s]] + [xg.at[me_s, :, lanes] for lanes in chunks]
+    far_refs = [far_bc] + [far_xg.at[:, lanes] for lanes in chunks]
+    for at in range(CHUNKS + 1):
         copy = pltpu.make_async_remote_copy(
-            src_ref=near.at[me_s],
-            dst_ref=far,
+            src_ref=near_refs[at],
+            dst_ref=far_refs[at],
             send_sem=raw_send.at[at],
             recv_sem=raw_recv.at[at],
             device_id=place(far_s, me_h, me_d),
@@ -289,8 +310,8 @@
         mt[2 * j] = mm(jnp.where(left, x_pair, zero_pair), gy_pair, NT)
         mt[2 * j + 1] = mm(jnp.where(left, zero_pair, x_pair), gy_pair, NT)
 
-    loads[4].wait()
-    loads[5].wait()
+    for load in loads[4:]:
+        load.wait()
     for copy in w_copies:
         copy.wait_recv()
     part[...] = mm(w_all[...], layer[...], NT)
@@ -374,15 +395,19 @@
     near_scale = jnp.where(first, to_end * dt, from_start)
     far_wide = widen(far_scale)
     near_wide = widen(near_scale)
-    for copy in raw_copies:
-        copy.wait_recv()
-    state = mm(
-        far_bc[...], (far_xg[...].astype(jnp.float32) * far_wide).astype(jnp.bfloat16), TN
-    ).astype(jnp.bfloat16)
-    carried = mm(bc[me_s], state, NN)
-    near = xg[me_s].astype(jnp.float32)
-    high, low = two_parts(near * carried)
-    w = mm(spread[:heads], high, NT) + mm(spread[:heads], low, NT)
+    raw_copies[0].wait_recv()
+    far_rows = far_bc[...]
+    near_rows = bc[me_s]
+    states, carried, inputs = [], [], []
+    w = jnp.zeros((heads, tokens), jnp.float32)
+    for c, lanes in enumerate(chunks):
+        raw_copies[c + 1].wait_recv()
+        scaled = far_xg[:, lanes].astype(jnp.float32) * far_wide[:, lanes]
+        states.append(mm(far_rows, scaled.astype(jnp.bfloat16), TN).astype(jnp.bfloat16))
+        carried.append(mm(near_rows, states[c], NN))
+        inputs.append(xg[me_s, :, lanes].astype(jnp.float32))
+        high, low = two_parts(inputs[c] * carried[c])
+        w = w + mm(spread[:heads, lanes], high, NT) + mm(spread[:heads, lanes], low, NT)
 
     v = to_end * w
     q = jnp.where(first, q + v, q)
@@ -410,17 +435,23 @@
 
     dt_wide = widen(dt)
     flag = jnp.where(first, 1.0, 0.0)
+    brought = jnp.concatenate(carried, axis=1)
     for j in range(heads // 2):
         lanes = slice(j * pair, (j + 1) * pair)
         gy_pair = xg[1, :, lanes]
         inner = jnp.where(left, mm(ke[2 * j], gy_pair, NN), mm(ke[2 * j + 1], gy_pair, NN))
         gx_ref[:, lanes] = (
-            inner * dt_wide[:, lanes] + flag * near_wide[:, lanes] * carried[:, lanes]
+            inner * dt_wide[:, lanes] + flag * near_wide[:, lanes] * brought[:, lanes]
         ).astype(jnp.bfloat16)
-    extra = mm((near * near_wide).astype(jnp.bfloat16), state, NT)
+    extra = jnp.zeros_like(dkt)
+    for c, lanes in enumerate(chunks):
+        extra = extra + mm((inputs[c] * near_wide[:, lanes]).astype(jnp.bfloat16), states[c], NT)
     dk = dkt.astype(jnp.bfloat16)
     gb_ref[...] = (mm(dk, bc[1], NN) + flag * extra).astype(jnp.bfloat16)
     gc_ref[...] = (mm(dk, bc[0], TN) + (1.0 - flag) * extra).astype(jnp.bfloat16)
+
+    for store in stores[:3]:
+        store.start()
 
     for copy in gp_copies:
         copy.wait_recv()
@@ -462,6 +493,7 @@
         term = mm(gp_all[rows, :], w_all[rows, :], TN)
         gin = gin + term.astype(jnp.bfloat16).astype(jnp.float32)
     gin_ref[...] = gin.astype(jnp.bfloat16)
+    stores[3].start()
 
     def arrived(k):
         spot = lax.rem(my_row + k, share)
@@ -481,6 +513,7 @@
     for k in range(1, share):
         gw = gw + gw_recv[k].astype(jnp.float32)
     gw_ref[...] = gw
+    stores[4].start()
 
     for copy in w_copies + raw_copies + part_copies + gp_copies:
         copy.wait_send()
@@ -489,6 +522,20 @@
             copy.wait_send()
         else:
             pl.when(away)(copy.wait_send)
+    for store in stores:
+        store.wait()
+
+
+def write_out(*refs):
+    sems = refs[-1]
+    count = len(refs) // 2
+    copies = [
+        pltpu.make_async_copy(refs[i], refs[count + i], sems.at[i]) for i in range(count)
+    ]
+    for copy in copies:
+        copy.start()
+    for copy in copies:
+        copy.wait()
 
 
 def fused_body(
@@ -503,9 +550,8 @@
     share = n_seq * n_dp
     b16, f32 = jnp.bfloat16, jnp.float32
     dma = pltpu.SemaphoreType.DMA
-    hbm = pl.BlockSpec(memory_space=pl.ANY)
-    vmem = pl.BlockSpec(memory_space=pltpu.VMEM)
-    gx, gb, gc, gin, gw = pl.pallas_call(
+    hbm = pl.BlockSpec(memory_space=pltpu.HBM)
+    results = pl.pallas_call(
         functools.partial(mixer_kernel, (n_seq, n_head, n_dp, heads, width // heads)),
         out_shape=(
             jax.ShapeDtypeStruct((tokens, width), b16),
@@ -514,9 +560,17 @@
             jax.ShapeDtypeStruct((tokens, feats), b16),
             jax.ShapeDtypeStruct((heads, rows_out), f32),
         ),
-        in_specs=[hbm] * 6 + [vmem] * 2,
-        out_specs=[vmem] * 5,
+        in_specs=[hbm] * 8,
+        out_specs=[hbm] * 5,
         scratch_shapes=[
+            pltpu.VMEM((tokens, width), b16),
+            pltpu.VMEM((tokens, state_size), b16),
+            pltpu.VMEM((tokens, state_size), b16),
+            pltpu.VMEM((tokens, feats), b16),
+            pltpu.VMEM((heads, rows_out), f32),
+            dma((5,)),
+            pltpu.VMEM((1, heads), f32),
+            pltpu.VMEM((1, heads), f32),
             pltpu.VMEM((tokens, feats), b16),
             pltpu.VMEM((2, tokens, width), b16),
             pltpu.VMEM((2, tokens, state_size), b16),
@@ -531,11 +585,11 @@
             pltpu.VMEM((n_head * heads, tokens), b16),
             pltpu.VMEM((n_head * heads, feats), b16),
             pltpu.VMEM((share, heads, rows_out), b16),
-            dma((6,)),
+            dma((8,)),
             dma((n_head - 1,)),
             dma((n_head - 1,)),
-            dma((2,)),
-            dma((2,)),
+            dma((CHUNKS + 1,)),
+            dma((CHUNKS + 1,)),
             dma((2 * n_head - 1,)),
             dma((2 * n_head - 1,)),
             dma((n_head - 1,)),
@@ -544,13 +598,23 @@
             dma((share,)),
         ],
         compiler_params=pltpu.CompilerParams(
-            collective_id=0, has_side_effects=True, vmem_limit_bytes=32 * 1024 * 1024
+            collective_id=0, has_side_effects=True, vmem_limit_bytes=60 * 1024 * 1024
         ),
         name="mixer",
     )(
         layer_input[0], head_input[0], in_matrix[0], out_matrix[0], grad_output[0],
         jnp.transpose(step_weight), step_bias[None], decay_log[None],
     )
+    count = len(results)
+    gx, gb, gc, gin, gw = pl.pallas_call(
+        write_out,
+        out_shape=tuple(jax.ShapeDtypeStruct(a.shape, a.dtype) for a in results),
+        in_specs=[pl.BlockSpec(memory_space=pl.ANY)] * count,
+        out_specs=[hbm] * count,
+        scratch_shapes=[dma((count,))],
+        compiler_params=pltpu.CompilerParams(vmem_limit_bytes=60 * 1024 * 1024),
+        name="write_out",
+    )(*results)
     return gx[None], gb[None], gc[None], gin[None], jnp.transpose(gw)
 
 

time: 34.6 us -> 46.6 us (1.35)
  Pallas kernels: 24.3 us -> 45.8 us
  local copies, waits for them, and re-layouts: 9.17 us -> 0 us
    pallas_call x0 -> x1, Pallas kernels: none -> 20 us  [fused_body(): pl.pallas_call(write_out, out_shape=tuple((jax.ShapeDtypeStruct(a.shape,...]
    unnamed x21 -> x0, local copies, waits for them, and re-layouts: 9.17 us -> none
    pallas_call x1, Pallas kernels: 24.3 us -> 25.8 us  [fused_body(): pl.pallas_call(functools.partial(mixer_kernel, (n_seq, n_head, n_dp, head...]
where the time goes in v2:
time: 46.6 us; the launch traced here: 46.4 us
  Pallas kernels  45.8 us (98%)
  between operations  0.64 us (1%)
    pallas_call x1, Pallas kernels, fused_body(): pl.pallas_call(functools.partial(mixer_kernel, (n_seq, n_head, n_dp, head...  25.8 us
    pallas_call x1, Pallas kernels, fused_body(): pl.pallas_call(write_out, out_shape=tuple((jax.ShapeDtypeStruct(a.shape,...  20 us

profile of v2, /device:TPU:0, one launch (start us, length us, event | category | flops | bytes accessed | tf_op | source)
XLA Modules:
  0.0 46.4 jit_solution(4832840063350354859)
XLA Ops:
  0.6 25.8 %mixer.1 = (bf16[128,1024]{1,0:T(8,128)(2,1)}, bf16[128,128]{1,0:T(8,128)(2,1)}, bf16[128,128]{1,0:T(8,128)(2,1)}, bf16[128,1024]{1,0:T(8,128)(2,1)}, f32[16,512]{1,0:T(8,128)}) custom-call(bf16[128,1024]{1,0:T(8,128)(2,1)} %bitcast.13, bf16[128,1024]{1,0:T(8,128)(2,1)} %bitcast.14, bf16[128,128]{1,0:T(8,128)(2,1)} %bitcast.17, bf16[128,128]{1,0:T(8,128)(2,1)} %bitcast.18, ...), custom_call_target="tpu_custom_call" | custom-call | tf_op jit(solution)/shard_map/mixer/pallas_call | solution.py:554
  26.4 20.0 %write_out.1 = (bf16[128,1024]{1,0:T(8,128)(2,1)}, bf16[128,128]{1,0:T(8,128)(2,1)}, bf16[128,128]{1,0:T(8,128)(2,1)}, bf16[128,1024]{1,0:T(8,128)(2,1)}, f32[16,512]{1,0:T(8,128)}) custom-call(bf16[128,1024]{1,0:T(8,128)(2,1)} %get-tuple-element.15.refs_0_, bf16[128,128]{1,0:T(8,128)(2,1)} %get-tuple-element.16.refs_1_, ...), custom_call_target="tpu_custom_call" | custom-call | tf_op jit(solution)/shard_map/write_out/pallas_call | solution.py:609

commit v3 on v2

--- a/solution.py
+++ b/solution.py
@@ -189,8 +189,7 @@
 def mixer_kernel(
     sizes,
     layer_hbm, x_hbm, b_hbm, c_hbm, gy_hbm, w_hbm, bias_hbm, rate_hbm,
-    gx_hbm, gb_hbm, gc_hbm, gin_hbm, gw_hbm,
-    gx_ref, gb_ref, gc_ref, gin_ref, gw_ref, out_sem,
+    gx_ref, gb_ref, gc_ref, gin_ref, gw_ref,
     bias_ref, rate_ref, layer, xg, bc, far_xg, far_bc, w_all, part, part_far, mt, ke, qcol, gp_all, gw_send, gw_recv,
     load_sem, w_send, w_recv, raw_send, raw_recv, p_send, p_recv, g_send, g_recv, d_send, d_recv,
 ):
@@ -207,19 +206,6 @@
 
     def place(s, h, d):
         return {"seq": s, "head": h, "dp": d}
-
-    stores = [
-        pltpu.make_async_copy(src, dst, out_sem.at[at])
-        for at, (src, dst) in enumerate(
-            (
-                (gx_ref, gx_hbm),
-                (gb_ref, gb_hbm),
-                (gc_ref, gc_hbm),
-                (gin_ref, gin_hbm),
-                (gw_ref, gw_hbm),
-            )
-        )
-    ]
 
     loads = [
         pltpu.make_async_copy(x_hbm, xg.at[0], load_sem.at[0]),
@@ -449,9 +435,6 @@
     dk = dkt.astype(jnp.bfloat16)
     gb_ref[...] = (mm(dk, bc[1], NN) + flag * extra).astype(jnp.bfloat16)
     gc_ref[...] = (mm(dk, bc[0], TN) + (1.0 - flag) * extra).astype(jnp.bfloat16)
-
-    for store in stores[:3]:
-        store.start()
 
     for copy in gp_copies:
         copy.wait_recv()
@@ -493,7 +476,6 @@
         term = mm(gp_all[rows, :], w_all[rows, :], TN)
         gin = gin + term.astype(jnp.bfloat16).astype(jnp.float32)
     gin_ref[...] = gin.astype(jnp.bfloat16)
-    stores[3].start()
 
     def arrived(k):
         spot = lax.rem(my_row + k, share)
@@ -513,7 +495,6 @@
     for k in range(1, share):
         gw = gw + gw_recv[k].astype(jnp.float32)
     gw_ref[...] = gw
-    stores[4].start()
 
     for copy in w_copies + raw_copies + part_copies + gp_copies:
         copy.wait_send()
@@ -522,8 +503,6 @@
             copy.wait_send()
         else:
             pl.when(away)(copy.wait_send)
-    for store in stores:
-        store.wait()
 
 
 def write_out(*refs):
@@ -554,21 +533,15 @@
     results = pl.pallas_call(
         functools.partial(mixer_kernel, (n_seq, n_head, n_dp, heads, width // heads)),
         out_shape=(
-            jax.ShapeDtypeStruct((tokens, width), b16),
-            jax.ShapeDtypeStruct((tokens, state_size), b16),
-            jax.ShapeDtypeStruct((tokens, state_size), b16),
-            jax.ShapeDtypeStruct((tokens, feats), b16),
-            jax.ShapeDtypeStruct((heads, rows_out), f32),
-        ),
-        in_specs=[hbm] * 8,
-        out_specs=[hbm] * 5,
-        scratch_shapes=[
             pltpu.VMEM((tokens, width), b16),
             pltpu.VMEM((tokens, state_size), b16),
             pltpu.VMEM((tokens, state_size), b16),
             pltpu.VMEM((tokens, feats), b16),
             pltpu.VMEM((heads, rows_out), f32),
-            dma((5,)),
+        ),
+        in_specs=[hbm] * 8,
+        out_specs=[pl.BlockSpec(memory_space=pltpu.VMEM)] * 5,
+        scratch_shapes=[
             pltpu.VMEM((1, heads), f32),
             pltpu.VMEM((1, heads), f32),
             pltpu.VMEM((tokens, feats), b16),
@@ -598,12 +571,17 @@
             dma((share,)),
         ],
         compiler_params=pltpu.CompilerParams(
-            collective_id=0, has_side_effects=True, vmem_limit_bytes=60 * 1024 * 1024
+            collective_id=0, has_side_effects=True, vmem_limit_bytes=32 * 1024 * 1024
         ),
         name="mixer",
     )(
-        layer_input[0], head_input[0], in_matrix[0], out_matrix[0], grad_output[0],
-        jnp.transpose(step_weight), step_bias[None], decay_log[None],
+        *(
+            pltpu.with_memory_space_constraint(a, pltpu.HBM)
+            for a in (
+                layer_input[0], head_input[0], in_matrix[0], out_matrix[0], grad_output[0],
+                jnp.transpose(step_weight), step_bias[None], decay_log[None],
+            )
+        )
     )
     count = len(results)
     gx, gb, gc, gin, gw = pl.pallas_call(
@@ -612,7 +590,6 @@
         in_specs=[pl.BlockSpec(memory_space=pl.ANY)] * count,
         out_specs=[hbm] * count,
         scratch_shapes=[dma((count,))],
-        compiler_params=pltpu.CompilerParams(vmem_limit_bytes=60 * 1024 * 1024),
         name="write_out",
     )(*results)
     return gx[None], gb[None], gc[None], gin[None], jnp.transpose(gw)

time: 46.6 us -> 49.2 us (1.056)
  local copies, waits for them, and re-layouts: 0 us -> 3.21 us
  Pallas kernels: 45.8 us -> 45.2 us
    unnamed x0 -> x10, local copies, waits for them, and re-layouts: none -> 3.21 us
    pallas_call x1, Pallas kernels: 25.8 us -> 25.1 us  [fused_body(): pl.pallas_call(functools.partial(mixer_kernel, (n_seq, n_head, n_dp, head...]
where the time goes in v3:
time: 49.2 us; the launch traced here: 49 us
  Pallas kernels  45.2 us (92%)
  local copies, waits for them, and re-layouts  3.21 us (7%)
  between operations  0.65 us (1%)
    pallas_call x1, Pallas kernels, fused_body(): pl.pallas_call(functools.partial(mixer_kernel, (n_seq, n_head, n_dp, head...  25.1 us
    pallas_call x1, Pallas kernels, fused_body(): pl.pallas_call(write_out, out_shape=tuple((jax.ShapeDtypeStruct(a.shape,...  20 us
    unnamed x10, local copies, waits for them, and re-layouts  3.21 us

profile of v3, /device:TPU:0, one launch (start us, length us, event | category | flops | bytes accessed | tf_op | source)
XLA Modules:
  0.0 49.0 jit_solution(17504113141004385890)
XLA Ops:
  0.6 25.1 %mixer.1 = (bf16[128,1024]{1,0:T(8,128)(2,1)S(1)}, bf16[128,128]{1,0:T(8,128)(2,1)S(1)}, bf16[128,128]{1,0:T(8,128)(2,1)S(1)}, bf16[128,1024]{1,0:T(8,128)(2,1)S(1)}, f32[16,512]{1,0:T(8,128)S(1)}) custom-call(bf16[128,1024]{1,0:T(8,128)(2,1)} %bitcast.13, bf16[128,1024]{1,0:T(8,128)(2,1)} %bitcast.14, bf16[128,128]{1,0:T(8,128)(2,1)} %bitcast.17, ...), custom_call_target="tpu_custom_call" | custom-call | tf_op jit(solution)/shard_map/mixer/pallas_call | solution.py:533
  25.8 0.0 copy-start
  25.8 0.7 %copy-done = bf16[128,1024]{1,0:T(8,128)(2,1)} copy-done((bf16[128,1024]{1,0:T(8,128)(2,1)}, bf16[128,1024]{1,0:T(8,128)(2,1)S(1)}, u32[]{:S(2)}) %copy-start) | copy-done | bytes 262168
  26.5 0.0 copy-start.1
  26.5 0.7 %copy-done.1 = bf16[128,1024]{1,0:T(8,128)(2,1)} copy-done((bf16[128,1024]{1,0:T(8,128)(2,1)}, bf16[128,1024]{1,0:T(8,128)(2,1)S(1)}, u32[]{:S(2)}) %copy-start.1) | copy-done | bytes 262168
  27.2 0.0 copy-start.2
  27.2 0.6 %copy-done.2 = bf16[128,128]{1,0:T(8,128)(2,1)} copy-done((bf16[128,128]{1,0:T(8,128)(2,1)}, bf16[128,128]{1,0:T(8,128)(2,1)S(1)}, u32[]{:S(2)}) %copy-start.2) | copy-done | bytes 32792
  27.8 0.0 copy-start.3
  27.8 0.6 %copy-done.3 = bf16[128,128]{1,0:T(8,128)(2,1)} copy-done((bf16[128,128]{1,0:T(8,128)(2,1)}, bf16[128,128]{1,0:T(8,128)(2,1)S(1)}, u32[]{:S(2)}) %copy-start.3) | copy-done | bytes 32792
  28.4 0.0 copy-start.4
  28.4 0.6 %copy-done.4 = f32[16,512]{1,0:T(8,128)} copy-done((f32[16,512]{1,0:T(8,128)}, f32[16,512]{1,0:T(8,128)S(1)}, u32[]{:S(2)}) %copy-start.4) | copy-done | bytes 32792
  29.0 20.0 %write_out.1 = (bf16[128,1024]{1,0:T(8,128)(2,1)}, bf16[128,128]{1,0:T(8,128)(2,1)}, bf16[128,128]{1,0:T(8,128)(2,1)}, bf16[128,1024]{1,0:T(8,128)(2,1)}, f32[16,512]{1,0:T(8,128)}) custom-call(bf16[128,1024]{1,0:T(8,128)(2,1)} %copy-done, bf16[128,128]{1,0:T(8,128)(2,1)} %copy-done.2, bf16[128,128]{1,0:T(8,128)(2,1)} %copy-done.3, ...), custom_call_target="tpu_custom_call" | custom-call | tf_op jit(solution)/shard_map/write_out/pallas_call | solution.py:587
Async XLA Ops:
  25.8 0.7 %copy-start = (bf16[128,1024]{1,0:T(8,128)(2,1)}, bf16[128,1024]{1,0:T(8,128)(2,1)S(1)}, u32[]{:S(2)}) copy-start(bf16[128,1024]{1,0:T(8,128)(2,1)S(1)} %get-tuple-element.15.refs_0_) | copy-start | bytes 786436
  26.5 0.7 %copy-start.1 = (bf16[128,1024]{1,0:T(8,128)(2,1)}, bf16[128,1024]{1,0:T(8,128)(2,1)S(1)}, u32[]{:S(2)}) copy-start(bf16[128,1024]{1,0:T(8,128)(2,1)S(1)} %get-tuple-element.18.refs_3_) | copy-start | bytes 786436
  27.2 0.6 %copy-start.2 = (bf16[128,128]{1,0:T(8,128)(2,1)}, bf16[128,128]{1,0:T(8,128)(2,1)S(1)}, u32[]{:S(2)}) copy-start(bf16[128,128]{1,0:T(8,128)(2,1)S(1)} %get-tuple-element.16.refs_1_) | copy-start | bytes 98308
  27.8 0.6 %copy-start.3 = (bf16[128,128]{1,0:T(8,128)(2,1)}, bf16[128,128]{1,0:T(8,128)(2,1)S(1)}, u32[]{:S(2)}) copy-start(bf16[128,128]{1,0:T(8,128)(2,1)S(1)} %get-tuple-element.17.refs_2_) | copy-start | bytes 98308
  28.4 0.6 %copy-start.4 = (f32[16,512]{1,0:T(8,128)}, f32[16,512]{1,0:T(8,128)S(1)}, u32[]{:S(2)}) copy-start(f32[16,512]{1,0:T(8,128)S(1)} %get-tuple-element.19.refs_4_) | copy-start | bytes 98308

commit v4 on v3

--- a/solution.py
+++ b/solution.py
@@ -590,8 +590,9 @@
         in_specs=[pl.BlockSpec(memory_space=pl.ANY)] * count,
         out_specs=[hbm] * count,
         scratch_shapes=[dma((count,))],
+        compiler_params=pltpu.CompilerParams(vmem_limit_bytes=4 * 1024 * 1024),
         name="write_out",
-    )(*results)
+    )(*(pltpu.with_memory_space_constraint(a, pltpu.VMEM) for a in results))
     return gx[None], gb[None], gc[None], gin[None], jnp.transpose(gw)
 
 

time: 49.2 us -> 26.8 us (0.54)
  Pallas kernels: 45.2 us -> 26 us
  local copies, waits for them, and re-layouts: 3.21 us -> 0 us
    pallas_call x1, Pallas kernels: 20 us -> 0.86 us  [fused_body(): pl.pallas_call(write_out, out_shape=tuple((jax.ShapeDtypeStruct(a.shape,...]
    unnamed x10 -> x0, local copies, waits for them, and re-layouts: 3.21 us -> none
where the time goes in v4:
time: 26.8 us; the launch traced here: 26.6 us
  Pallas kernels  26 us (97%)
  between operations  0.64 us (2%)
    pallas_call x1, Pallas kernels, fused_body(): pl.pallas_call(functools.partial(mixer_kernel, (n_seq, n_head, n_dp, head...  25.1 us
    pallas_call x1, Pallas kernels, fused_body(): pl.pallas_call(write_out, out_shape=tuple((jax.ShapeDtypeStruct(a.shape,...  0.86 us

profile of v4, /device:TPU:0, one launch (start us, length us, event | category | flops | bytes accessed | tf_op | source)
XLA Modules:
  0.0 26.6 jit_solution(6311110165214562508)
XLA Ops:
  0.6 25.1 %mixer.1 = (bf16[128,1024]{1,0:T(8,128)(2,1)S(1)}, bf16[128,128]{1,0:T(8,128)(2,1)S(1)}, bf16[128,128]{1,0:T(8,128)(2,1)S(1)}, bf16[128,1024]{1,0:T(8,128)(2,1)S(1)}, f32[16,512]{1,0:T(8,128)S(1)}) custom-call(bf16[128,1024]{1,0:T(8,128)(2,1)} %bitcast.13, bf16[128,1024]{1,0:T(8,128)(2,1)} %bitcast.14, bf16[128,128]{1,0:T(8,128)(2,1)} %bitcast.17, ...), custom_call_target="tpu_custom_call" | custom-call | tf_op jit(solution)/shard_map/mixer/pallas_call | solution.py:533
  25.8 0.9 %write_out.1 = (bf16[128,1024]{1,0:T(8,128)(2,1)}, bf16[128,128]{1,0:T(8,128)(2,1)}, bf16[128,128]{1,0:T(8,128)(2,1)}, bf16[128,1024]{1,0:T(8,128)(2,1)}, f32[16,512]{1,0:T(8,128)}) custom-call(bf16[128,1024]{1,0:T(8,128)(2,1)S(1)} %get-tuple-element.15.refs_0_, bf16[128,128]{1,0:T(8,128)(2,1)S(1)} %get-tuple-element.16.refs_1_, ...), custom_call_target="tpu_custom_call" | custom-call | tf_op jit(solution)/shard_map/write_out/pallas_call | solution.py:587

commit v5 on v4

--- a/solution.py
+++ b/solution.py
@@ -283,8 +283,9 @@
             device_id=place(far_s, me_h, me_d),
             device_id_type=MESH,
         )
+        raw_copies.append(copy)
+    for copy in raw_copies[: 1 + CHUNKS // 2]:
         copy.start()
-        raw_copies.append(copy)
 
     pair = 2 * p_size
     left = lax.broadcasted_iota(jnp.int32, (tokens, pair), 1) < p_size
@@ -318,6 +319,8 @@
             )
             copy.start()
             part_copies.append(copy)
+    for copy in raw_copies[1 + CHUNKS // 2 :]:
+        copy.start()
 
     upper = (
         lax.broadcasted_iota(jnp.int32, (tokens, tokens), 0)
@@ -354,6 +357,22 @@
     dkt = jnp.zeros((tokens, tokens), jnp.float32)
     r_rows = []
     for h in range(heads):
+        if h == heads // 2:
+            first = me_s == 0
+            for k in range(n_head):
+                part_copies[2 * k].wait_recv()
+            far_pre = bias
+            for k in range(n_head):
+                far_pre = far_pre + part_far[2 * k]
+            far_dt = softplus(far_pre)
+            far_cum = exact_mm(-rate * far_dt, summing)
+            far_total = far_cum[:, tokens - 1 :]
+            from_start = jnp.exp(cum)
+            to_end = jnp.exp(total - cum)
+            far_scale = jnp.where(first, jnp.exp(far_cum), jnp.exp(far_total - far_cum) * far_dt)
+            near_scale = jnp.where(first, to_end * dt, from_start)
+            far_wide = widen(far_scale)
+            near_wide = widen(near_scale)
         gap = cum[h : h + 1, :] - cum_col[:, h : h + 1]
         span = jnp.exp(jnp.where(upper, gap, -1e30))
         ke[h] = (kt * span).astype(jnp.bfloat16)
@@ -366,28 +385,13 @@
     r = jnp.concatenate(r_rows, axis=0)
     q = jnp.transpose(qcol[...])[:heads]
 
-    first = me_s == 0
-    for k in range(n_head):
-        part_copies[2 * k].wait_recv()
-    far_pre = bias
-    for k in range(n_head):
-        far_pre = far_pre + part_far[2 * k]
-    far_dt = softplus(far_pre)
-    far_cum = exact_mm(-rate * far_dt, summing)
-    far_total = far_cum[:, tokens - 1 :]
-    from_start = jnp.exp(cum)
-    to_end = jnp.exp(total - cum)
-    far_scale = jnp.where(first, jnp.exp(far_cum), jnp.exp(far_total - far_cum) * far_dt)
-    near_scale = jnp.where(first, to_end * dt, from_start)
-    far_wide = widen(far_scale)
-    near_wide = widen(near_scale)
-    raw_copies[0].wait_recv()
+    for copy in raw_copies:
+        copy.wait_recv()
     far_rows = far_bc[...]
     near_rows = bc[me_s]
     states, carried, inputs = [], [], []
     w = jnp.zeros((heads, tokens), jnp.float32)
     for c, lanes in enumerate(chunks):
-        raw_copies[c + 1].wait_recv()
         scaled = far_xg[:, lanes].astype(jnp.float32) * far_wide[:, lanes]
         states.append(mm(far_rows, scaled.astype(jnp.bfloat16), TN).astype(jnp.bfloat16))
         carried.append(mm(near_rows, states[c], NN))
@@ -429,12 +433,6 @@
         gx_ref[:, lanes] = (
             inner * dt_wide[:, lanes] + flag * near_wide[:, lanes] * brought[:, lanes]
         ).astype(jnp.bfloat16)
-    extra = jnp.zeros_like(dkt)
-    for c, lanes in enumerate(chunks):
-        extra = extra + mm((inputs[c] * near_wide[:, lanes]).astype(jnp.bfloat16), states[c], NT)
-    dk = dkt.astype(jnp.bfloat16)
-    gb_ref[...] = (mm(dk, bc[1], NN) + flag * extra).astype(jnp.bfloat16)
-    gc_ref[...] = (mm(dk, bc[0], TN) + (1.0 - flag) * extra).astype(jnp.bfloat16)
 
     for copy in gp_copies:
         copy.wait_recv()
@@ -469,6 +467,13 @@
                 @pl.when(jnp.logical_not(away))
                 def _():
                     gw_recv[my_row] = block[...]
+
+    extra = jnp.zeros_like(dkt)
+    for c, lanes in enumerate(chunks):
+        extra = extra + mm((inputs[c] * near_wide[:, lanes]).astype(jnp.bfloat16), states[c], NT)
+    dk = dkt.astype(jnp.bfloat16)
+    gb_ref[...] = (mm(dk, bc[1], NN) + flag * extra).astype(jnp.bfloat16)
+    gc_ref[...] = (mm(dk, bc[0], TN) + (1.0 - flag) * extra).astype(jnp.bfloat16)
 
     gin = jnp.zeros((tokens, feats), jnp.float32)
     for j in range(n_head):

time: 26.8 us -> 25.4 us (0.948)
  Pallas kernels: 26 us -> 24.6 us
    pallas_call x1, Pallas kernels: 25.1 us -> 23.8 us  [fused_body(): pl.pallas_call(functools.partial(mixer_kernel, (n_seq, n_head, n_dp, head...]
where the time goes in v5:
time: 25.4 us; the launch traced here: 25.3 us
  Pallas kernels  24.6 us (97%)
  between operations  0.64 us (3%)
    pallas_call x1, Pallas kernels, fused_body(): pl.pallas_call(functools.partial(mixer_kernel, (n_seq, n_head, n_dp, head...  23.8 us
    pallas_call x1, Pallas kernels, fused_body(): pl.pallas_call(write_out, out_shape=tuple((jax.ShapeDtypeStruct(a.shape,...  0.86 us

profile of v5, /device:TPU:0, one launch (start us, length us, event | category | flops | bytes accessed | tf_op | source)
XLA Modules:
  0.0 25.3 jit_solution(14788014683362354307)
XLA Ops:
  0.6 23.8 %mixer.1 = (bf16[128,1024]{1,0:T(8,128)(2,1)S(1)}, bf16[128,128]{1,0:T(8,128)(2,1)S(1)}, bf16[128,128]{1,0:T(8,128)(2,1)S(1)}, bf16[128,1024]{1,0:T(8,128)(2,1)S(1)}, f32[16,512]{1,0:T(8,128)S(1)}) custom-call(bf16[128,1024]{1,0:T(8,128)(2,1)} %bitcast.13, bf16[128,1024]{1,0:T(8,128)(2,1)} %bitcast.14, bf16[128,128]{1,0:T(8,128)(2,1)} %bitcast.17, ...), custom_call_target="tpu_custom_call" | custom-call | tf_op jit(solution)/shard_map/mixer/pallas_call | solution.py:538
  24.4 0.9 %write_out.1 = (bf16[128,1024]{1,0:T(8,128)(2,1)}, bf16[128,128]{1,0:T(8,128)(2,1)}, bf16[128,128]{1,0:T(8,128)(2,1)}, bf16[128,1024]{1,0:T(8,128)(2,1)}, f32[16,512]{1,0:T(8,128)}) custom-call(bf16[128,1024]{1,0:T(8,128)(2,1)S(1)} %get-tuple-element.15.refs_0_, bf16[128,128]{1,0:T(8,128)(2,1)S(1)} %get-tuple-element.16.refs_1_, ...), custom_call_target="tpu_custom_call" | custom-call | tf_op jit(solution)/shard_map/write_out/pallas_call | solution.py:592

commit v6 on v5

--- a/solution.py
+++ b/solution.py
@@ -170,10 +170,14 @@
     return lax.dot_general(a, b, dims, preferred_element_type=jnp.float32)
 
 
-def exact_mm(a, b):
-    return lax.dot_general(
-        a, b, NN, precision=lax.Precision.HIGHEST, preferred_element_type=jnp.float32
-    )
+def exact_mm(a, ones):
+    count = a.shape[0]
+    parts = []
+    for _ in range(3):
+        parts.append(a.astype(jnp.bfloat16))
+        a = a - parts[-1].astype(jnp.float32)
+    sums = mm(jnp.concatenate(parts, axis=0), ones, NN)
+    return sums[:count] + (sums[count : 2 * count] + sums[2 * count :])
 
 
 def two_parts(v):
@@ -221,8 +225,6 @@
         pltpu.make_async_copy(bias_hbm, bias_ref, load_sem.at[6]),
         pltpu.make_async_copy(rate_hbm, rate_ref, load_sem.at[7]),
     ]
-    for load in loads:
-        load.start()
 
     barrier = pltpu.get_barrier_semaphore()
     my_row = me_s * n_dp + me_d
@@ -251,6 +253,8 @@
             greet()
         else:
             pl.when(jnp.logical_not(mine))(greet)
+    for load in loads:
+        load.start()
     pl.semaphore_wait(barrier, 2 * n_head - 1 + share - jnp.where(mine, 1, 0))
 
     w_copies = []
@@ -297,17 +301,43 @@
         mt[2 * j] = mm(jnp.where(left, x_pair, zero_pair), gy_pair, NT)
         mt[2 * j + 1] = mm(jnp.where(left, zero_pair, x_pair), gy_pair, NT)
 
+    upper = (
+        lax.broadcasted_iota(jnp.int32, (tokens, tokens), 0)
+        <= lax.broadcasted_iota(jnp.int32, (tokens, tokens), 1)
+    )
+    summing = jnp.where(upper, 1.0, 0.0).astype(jnp.bfloat16)
+    lower = jnp.where(
+        lax.broadcasted_iota(jnp.int32, (tokens, tokens), 0)
+        >= lax.broadcasted_iota(jnp.int32, (tokens, tokens), 1),
+        1.0,
+        0.0,
+    ).astype(jnp.bfloat16)
+    square = lax.broadcasted_iota(jnp.int32, (heads, heads), 0) == lax.broadcasted_iota(
+        jnp.int32, (heads, heads), 1
+    )
+
+    def column(row):
+        return jnp.sum(jnp.where(square, row, 0.0), axis=1, keepdims=True)
+
+    spread_rows = lax.rem(lax.broadcasted_iota(jnp.int32, (2 * heads, heads * p_size), 0), heads)
+    spread_at = lax.broadcasted_iota(jnp.int32, (2 * heads, heads * p_size), 1) // p_size
+    spread = jnp.where(spread_rows == spread_at, 1.0, 0.0).astype(jnp.bfloat16)
+
+    def widen(v):
+        high, low = two_parts(v)
+        return mm(jnp.concatenate([high, low], axis=0), spread, TN)
+
     for load in loads[4:]:
         load.wait()
+    bias = column(bias_ref[...])
+    rate = jnp.exp(column(rate_ref[...]))
     for copy in w_copies:
         copy.wait_recv()
     part[...] = mm(w_all[...], layer[...], NT)
-    part_copies = []
-    for k in range(n_head):
-        to = head_at(k)
-        for hop in range(2):
-            if k == 0 and hop == 0:
-                continue
+    part_copies = {}
+    for hop in range(2):
+        for k in range(1 - hop, n_head):
+            to = head_at(k)
             at = 2 * k + hop - 1
             copy = pltpu.make_async_remote_copy(
                 src_ref=part.at[pl.ds(pl.multiple_of(to * heads, heads), heads)],
@@ -318,31 +348,9 @@
                 device_id_type=MESH,
             )
             copy.start()
-            part_copies.append(copy)
+            part_copies[at] = copy
     for copy in raw_copies[1 + CHUNKS // 2 :]:
         copy.start()
-
-    upper = (
-        lax.broadcasted_iota(jnp.int32, (tokens, tokens), 0)
-        <= lax.broadcasted_iota(jnp.int32, (tokens, tokens), 1)
-    )
-    summing = upper.astype(jnp.float32)
-    square = lax.broadcasted_iota(jnp.int32, (heads, heads), 0) == lax.broadcasted_iota(
-        jnp.int32, (heads, heads), 1
-    )
-
-    def column(row):
-        return jnp.sum(jnp.where(square, row, 0.0), axis=1, keepdims=True)
-
-    bias = column(bias_ref[...])
-    rate = jnp.exp(column(rate_ref[...]))
-    spread_rows = lax.rem(lax.broadcasted_iota(jnp.int32, (2 * heads, heads * p_size), 0), heads)
-    spread_at = lax.broadcasted_iota(jnp.int32, (2 * heads, heads * p_size), 1) // p_size
-    spread = jnp.where(spread_rows == spread_at, 1.0, 0.0).astype(jnp.bfloat16)
-
-    def widen(v):
-        high, low = two_parts(v)
-        return mm(jnp.concatenate([high, low], axis=0), spread, TN)
 
     for k in range(1, n_head):
         part_copies[2 * k - 1].wait_recv()
@@ -403,10 +411,6 @@
     q = jnp.where(first, q + v, q)
     da = r - dt * q + jnp.where(first, 0.0, from_start * w)
     at_end = jnp.where(first, jnp.sum(dt * v, axis=1, keepdims=True), 0.0)
-    lower = (
-        lax.broadcasted_iota(jnp.int32, (tokens, tokens), 0)
-        >= lax.broadcasted_iota(jnp.int32, (tokens, tokens), 1)
-    ).astype(jnp.float32)
     grad_step = q - rate * (exact_mm(da, lower) + at_end)
     my_rows = pl.ds(pl.multiple_of(me_h * heads, heads), heads)
     gp_all[my_rows, :] = (grad_step * jax.nn.sigmoid(preact)).astype(jnp.bfloat16)
@@ -501,7 +505,7 @@
         gw = gw + gw_recv[k].astype(jnp.float32)
     gw_ref[...] = gw
 
-    for copy in w_copies + raw_copies + part_copies + gp_copies:
+    for copy in w_copies + raw_copies + list(part_copies.values()) + gp_copies:
         copy.wait_send()
     for copy, away in gw_copies:
         if away is None:

time: 25.4 us -> 25.5 us (level)
  no operation moved by 1% of the time
where the time goes in v6:
time: 25.5 us; the launch traced here: 25.3 us
  Pallas kernels  24.7 us (97%)
  between operations  0.64 us (3%)
    pallas_call x1, Pallas kernels, fused_body(): pl.pallas_call(functools.partial(mixer_kernel, (n_seq, n_head, n_dp, head...  23.8 us
    pallas_call x1, Pallas kernels, fused_body(): pl.pallas_call(write_out, out_shape=tuple((jax.ShapeDtypeStruct(a.shape,...  0.86 us

profile of v6, /device:TPU:0, one launch (start us, length us, event | category | flops | bytes accessed | tf_op | source)
XLA Modules:
  0.0 25.3 jit_solution(13247065656175832880)
XLA Ops:
  0.6 23.8 %mixer.1 = (bf16[128,1024]{1,0:T(8,128)(2,1)S(1)}, bf16[128,128]{1,0:T(8,128)(2,1)S(1)}, bf16[128,128]{1,0:T(8,128)(2,1)S(1)}, bf16[128,1024]{1,0:T(8,128)(2,1)S(1)}, f32[16,512]{1,0:T(8,128)S(1)}) custom-call(bf16[128,1024]{1,0:T(8,128)(2,1)} %bitcast.13, bf16[128,1024]{1,0:T(8,128)(2,1)} %bitcast.14, bf16[128,128]{1,0:T(8,128)(2,1)} %bitcast.17, ...), custom_call_target="tpu_custom_call" | custom-call | tf_op jit(solution)/shard_map/mixer/pallas_call | solution.py:542
  24.5 0.9 %write_out.1 = (bf16[128,1024]{1,0:T(8,128)(2,1)}, bf16[128,128]{1,0:T(8,128)(2,1)}, bf16[128,128]{1,0:T(8,128)(2,1)}, bf16[128,1024]{1,0:T(8,128)(2,1)}, f32[16,512]{1,0:T(8,128)}) custom-call(bf16[128,1024]{1,0:T(8,128)(2,1)S(1)} %get-tuple-element.15.refs_0_, bf16[128,128]{1,0:T(8,128)(2,1)S(1)} %get-tuple-element.16.refs_1_, ...), custom_call_target="tpu_custom_call" | custom-call | tf_op jit(solution)/shard_map/write_out/pallas_call | solution.py:596

commit v7 on v6

--- a/solution.py
+++ b/solution.py
@@ -288,7 +288,7 @@
             device_id_type=MESH,
         )
         raw_copies.append(copy)
-    for copy in raw_copies[: 1 + CHUNKS // 2]:
+    for copy in raw_copies[:CHUNKS]:
         copy.start()
 
     pair = 2 * p_size
@@ -349,7 +349,7 @@
             )
             copy.start()
             part_copies[at] = copy
-    for copy in raw_copies[1 + CHUNKS // 2 :]:
+    for copy in raw_copies[CHUNKS:]:
         copy.start()
 
     for k in range(1, n_head):
@@ -393,13 +393,15 @@
     r = jnp.concatenate(r_rows, axis=0)
     q = jnp.transpose(qcol[...])[:heads]
 
-    for copy in raw_copies:
-        copy.wait_recv()
+    raw_copies[0].wait_recv()
     far_rows = far_bc[...]
     near_rows = bc[me_s]
     states, carried, inputs = [], [], []
     w = jnp.zeros((heads, tokens), jnp.float32)
     for c, lanes in enumerate(chunks):
+        if c % (CHUNKS // 2) == 0:
+            for copy in raw_copies[1 + c : 1 + c + CHUNKS // 2]:
+                copy.wait_recv()
         scaled = far_xg[:, lanes].astype(jnp.float32) * far_wide[:, lanes]
         states.append(mm(far_rows, scaled.astype(jnp.bfloat16), TN).astype(jnp.bfloat16))
         carried.append(mm(near_rows, states[c], NN))

time: 25.5 us -> 25.7 us (level)
  no operation moved by 1% of the time
where the time goes in v7:
time: 25.7 us; the launch traced here: 25.6 us
  Pallas kernels  24.9 us (97%)
  between operations  0.64 us (2%)
    pallas_call x1, Pallas kernels, fused_body(): pl.pallas_call(functools.partial(mixer_kernel, (n_seq, n_head, n_dp, head...  24.1 us
    pallas_call x1, Pallas kernels, fused_body(): pl.pallas_call(write_out, out_shape=tuple((jax.ShapeDtypeStruct(a.shape,...  0.86 us

profile of v7, /device:TPU:0, one launch (start us, length us, event | category | flops | bytes accessed | tf_op | source)
XLA Modules:
  0.0 25.6 jit_solution(14664479122749827639)
XLA Ops:
  0.6 24.1 %mixer.1 = (bf16[128,1024]{1,0:T(8,128)(2,1)S(1)}, bf16[128,128]{1,0:T(8,128)(2,1)S(1)}, bf16[128,128]{1,0:T(8,128)(2,1)S(1)}, bf16[128,1024]{1,0:T(8,128)(2,1)S(1)}, f32[16,512]{1,0:T(8,128)S(1)}) custom-call(bf16[128,1024]{1,0:T(8,128)(2,1)} %bitcast.13, bf16[128,1024]{1,0:T(8,128)(2,1)} %bitcast.14, bf16[128,128]{1,0:T(8,128)(2,1)} %bitcast.17, ...), custom_call_target="tpu_custom_call" | custom-call | tf_op jit(solution)/shard_map/mixer/pallas_call | solution.py:544
  24.7 0.9 %write_out.1 = (bf16[128,1024]{1,0:T(8,128)(2,1)}, bf16[128,128]{1,0:T(8,128)(2,1)}, bf16[128,128]{1,0:T(8,128)(2,1)}, bf16[128,1024]{1,0:T(8,128)(2,1)}, f32[16,512]{1,0:T(8,128)}) custom-call(bf16[128,1024]{1,0:T(8,128)(2,1)S(1)} %get-tuple-element.15.refs_0_, bf16[128,128]{1,0:T(8,128)(2,1)S(1)} %get-tuple-element.16.refs_1_, ...), custom_call_target="tpu_custom_call" | custom-call | tf_op jit(solution)/shard_map/write_out/pallas_call | solution.py:598
